TPU v7x, 128 devices: a whole 4x4x4 slice. The times are simulated.
128 devices in a mesh: dp: 8 (over z, core), seq: 16 (over y, x).
Axes of the slice: x: 4, y: 4, z: 4, core: 2. Of those that a mesh axis runs over, the one named last changes fastest.
Arguments:
- queries: bfloat16 [16, 2048, 2048], P('dp', 'seq'), may hold values from -6 to 6
- d_context: bfloat16 [16, 2048, 2048], P('dp', 'seq'), may hold values from -12 to 12
- database: bfloat16 [2048, 128, 896], P(('dp', 'seq')), may hold values from -6 to 6
- key_weight: bfloat16 [896, 2048], replicated, may hold values from -0.1875 to 0.1875
- value_weight: bfloat16 [896, 2048], replicated, may hold values from -0.1875 to 0.1875
- neighbour_shard: int32 [8, 16, 4, 2], P('dp', 'seq'), may hold values from 0 to 7, all different within a row; in each aligned block of 4 rows (0 to 3, 4 to 7, ..., all dimensions but the last counted through in order) at most 2 rows name the same one
- neighbour_row: int32 [8, 16, 4, 2], P('dp', 'seq'), may hold values from 0 to 15
Outputs:
- context: bfloat16 [16, 2048, 2048], P('dp', 'seq')
- query_grad: bfloat16 [16, 2048, 2048], P('dp', 'seq')
- database_grad: float32 [2048, 128, 896], P(('dp', 'seq'))
- key_weight_grad: float32 [896, 2048], P(('dp', 'seq'))
- value_weight_grad: float32 [896, 2048], P(('dp', 'seq'))
Inputs may be any that keep to these rules, and one draw needn't show every extreme that they name: `neighbour_shard`: among the 4 rows of one device (aligned blocks of the first three dimensions taken together), no shard is named more than 2 times, a bound that some block reaches; the 2 neighbours of one block name different shards.
All inputs are finite; a program needn't handle non-finite values.
Results may differ from a plain program's by a relative error of at most 0.015.
Values may be sent and summed in bfloat16 or wider, within the bound.
A program may use at most 192 MiB of HBM per device.

v0:
```python
import jax
import jax.numpy as jnp
from jax import lax
from jax.sharding import PartitionSpec as P

HD = 128
ENC = 896
SPAN = 64
NB_LEN = 128


def shifted(array, axis, by):
    count = lax.axis_size(axis)
    pairs = [(i, i + by) for i in range(count) if 0 <= i + by < count]
    return lax.ppermute(array, axis, pairs)


def local(queries, d_context, database, key_weight, value_weight, neighbour_shard, neighbour_row):
    seq_count, seq_span, feat_width = queries.shape
    head_count = feat_width // HD
    lag_rows = SPAN - 1
    block_count = seq_count * seq_span // SPAN
    pick_count = neighbour_shard.shape[-1]
    ref_count = block_count * pick_count
    shard_count = lax.axis_size("dp")
    capacity = 2 * ref_count // shard_count
    slot_count = shard_count * capacity
    near_len = pick_count * NB_LEN
    target = neighbour_shard.reshape(ref_count)
    wanted = neighbour_row.reshape(ref_count)
    owners = (target[:, None] == jnp.arange(shard_count, dtype=jnp.int32)[None, :]).astype(
        jnp.int32
    )
    before = jnp.cumsum(owners, axis=0) - owners
    slot_rank = jnp.sum(before * owners, axis=1)
    slot_index = target * capacity + slot_rank
    placed = (slot_index[:, None] == jnp.arange(slot_count, dtype=jnp.int32)[None, :]).astype(
        jnp.int32
    )
    request = jnp.sum(placed * wanted[:, None], axis=0)
    arrived = lax.all_to_all(request, "dp", split_axis=0, concat_axis=0, tiled=True)
    outgoing = jnp.take(database, arrived, axis=0)
    incoming = lax.all_to_all(outgoing, "dp", split_axis=0, concat_axis=0, tiled=True)
    neighbours = jnp.take(incoming, slot_index, axis=0).reshape(ref_count * NB_LEN, ENC)
    key_rows = jnp.dot(neighbours, key_weight, preferred_element_type=jnp.float32).astype(
        jnp.bfloat16
    )
    value_rows = jnp.dot(neighbours, value_weight, preferred_element_type=jnp.float32).astype(
        jnp.bfloat16
    )
    key_heads = key_rows.reshape(block_count, near_len, head_count, HD)
    value_heads = value_rows.reshape(block_count, near_len, head_count, HD)
    head_rows, head_grads = shifted((queries[:, :lag_rows], d_context[:, :lag_rows]), "seq", -1)
    query_blocks = jnp.concatenate([queries[:, lag_rows:], head_rows], axis=1).reshape(
        block_count, SPAN, head_count, HD
    )
    grad_blocks = jnp.concatenate([d_context[:, lag_rows:], head_grads], axis=1).reshape(
        block_count, SPAN, head_count, HD
    )
    score_scale = HD ** (-0.5)
    scores = (
        jnp.einsum("cqhd,ckhd->chqk", query_blocks, key_heads, preferred_element_type=jnp.float32)
        * score_scale
    )
    weights = jnp.exp(scores)
    weights = weights / jnp.sum(weights, axis=-1, keepdims=True)
    weight_half = weights.astype(jnp.bfloat16)
    context_shift = jnp.einsum(
        "chqk,ckhd->cqhd", weight_half, value_heads, preferred_element_type=jnp.float32
    )
    context_shift = context_shift.astype(jnp.bfloat16).reshape(seq_count, seq_span, feat_width)
    prob_grads = jnp.einsum(
        "cqhd,ckhd->chqk", grad_blocks, value_heads, preferred_element_type=jnp.float32
    )
    row_delta = jnp.sum(weights * prob_grads, axis=-1, keepdims=True)
    score_grads = (score_scale * weights * (prob_grads - row_delta)).astype(jnp.bfloat16)
    query_shift = jnp.einsum(
        "chqk,ckhd->cqhd", score_grads, key_heads, preferred_element_type=jnp.float32
    )
    query_shift = query_shift.astype(jnp.bfloat16).reshape(seq_count, seq_span, feat_width)
    key_grads = jnp.einsum(
        "chqk,cqhd->ckhd", score_grads, query_blocks, preferred_element_type=jnp.float32
    )
    key_grads = key_grads.astype(jnp.bfloat16).reshape(ref_count * NB_LEN, feat_width)
    value_grads = jnp.einsum(
        "chqk,cqhd->ckhd", weight_half, grad_blocks, preferred_element_type=jnp.float32
    )
    value_grads = value_grads.astype(jnp.bfloat16).reshape(ref_count * NB_LEN, feat_width)
    proj_grads = jnp.concatenate([key_grads, value_grads], axis=1)
    both_weights = jnp.concatenate([key_weight, value_weight], axis=1)
    near_grads = jnp.einsum(
        "pz,xz->px", proj_grads, both_weights, preferred_element_type=jnp.float32
    )
    near_grads = near_grads.reshape(ref_count, NB_LEN * ENC)
    slot_grads = jnp.einsum(
        "rs,rx->sx", placed.astype(jnp.float32), near_grads, precision=lax.Precision.HIGHEST
    )
    returned = lax.all_to_all(
        slot_grads.reshape(slot_count, NB_LEN, ENC).astype(jnp.bfloat16),
        "dp",
        split_axis=0,
        concat_axis=0,
        tiled=True,
    ).astype(jnp.float32)
    row_hits = (jnp.arange(database.shape[0], dtype=jnp.int32)[:, None] == arrived[None, :]).astype(
        jnp.float32
    )
    database_grad = jnp.einsum(
        "rs,sx->rx",
        row_hits,
        returned.reshape(slot_count, NB_LEN * ENC),
        precision=lax.Precision.HIGHEST,
    )
    database_grad = database_grad.reshape(database.shape)
    keep_rows = seq_span - lag_rows
    prior_context, prior_grads = shifted(
        (context_shift[:, keep_rows:], query_shift[:, keep_rows:]), "seq", 1
    )
    context = jnp.concatenate([prior_context, context_shift[:, :keep_rows]], axis=1)
    query_grad = jnp.concatenate([prior_grads, query_shift[:, :keep_rows]], axis=1)
    owned_grads = lax.psum_scatter(
        jnp.einsum("px,pz->xz", neighbours, proj_grads, preferred_element_type=jnp.float32),
        ("dp", "seq"),
        scatter_dimension=0,
        tiled=True,
    )
    return (
        context,
        query_grad,
        database_grad,
        owned_grads[:, :feat_width],
        owned_grads[:, feat_width:],
    )


def solution(mesh):
    return jax.shard_map(
        local,
        mesh=mesh,
        in_specs=(
            P("dp", "seq", None),
            P("dp", "seq", None),
            P(("dp", "seq"), None, None),
            P(),
            P(),
            P("dp", "seq", None, None),
            P("dp", "seq", None, None),
        ),
        out_specs=(
            P("dp", "seq", None),
            P("dp", "seq", None),
            P(("dp", "seq"), None, None),
            P(("dp", "seq"), None),
            P(("dp", "seq"), None),
        ),
        check_vma=False,
    )
```

profile of v0, /device:TPU:1, one launch (start us, length us, event | category | flops | bytes accessed | tf_op | source)
XLA Modules:
  0.0 358.5 jit_solution(8209220344046602530)
XLA Ops:
  9.3 11.2 %all_to_all.25 = s32[8,2,1]{1,2,0:T(1,128)S(1)} all-to-all(s32[8,2,1]{1,2,0:T(1,128)S(1)} %bitcast.95), channel_id=1, replica_groups=mesh['dp'=8,'seq'=16] {'dp'}, dimensions={0} | all-to-all | bytes 128 | tf_op jit(solution)/shard_map/all_to_all | solution.py:41
  21.9 4.8 %gather_fusion = bf16[16,128,896]{2,1,0:T(8,128)(2,1)} fusion(bf16[16,128,896]{2,1,0:T(8,128)(2,1)} %param.9, s32[1024]{0:T(1024)S(1)} %pad_clamp_fusion.1), kind=kCustom, calls=%fused_computation | custom fusion | bytes 7340096 | tf_op jit(solution)/shard_map/jit(_take)/gather | solution.py:42
  26.7 4.3 %broadcast_select_fusion = bf16[16,128,896]{2,1,0:T(8,128)(2,1)} fusion(bf16[16,128,896]{2,1,0:T(8,128)(2,1)} %gather_fusion, pred[16]{0:T(512)(128)(4,1)S(1)} %compare_and_fusion), kind=kLoop, calls=%fused_computation.28 | loop fusion | flops 1835008 | bytes 7340048 | tf_op jit(solution)/shard_map/jit(_take)/select_n | solution.py:42
  31.0 5.2 %all-to-all-start.1 = ((bf16[16,128,896]{2,1,0:T(8,128)(2,1)}), bf16[16,128,896]{2,1,0:T(8,128)(2,1)}, u32[]{:S(2)}, u32[]{:S(2)}) async-start(bf16[16,128,896]{2,1,0:T(8,128)(2,1)} %broadcast_select_fusion), calls=%async_computation.1 | async-start | bytes 7340032 | tf_op jit(solution)/shard_map/all_to_all | solution.py:43
  40.3 11.3 %collective-permute-done = bf16[2,63,2048]{2,1,0:T(8,128)(2,1)S(1)} collective-permute-done((bf16[2,63,2048]{2,1,0:T(8,128)(2,1)S(1)}, bf16[2,63,2048]{2,1,0:T(8,128)(2,1)S(1)}, u32[]{:S(2)}, u32[]{:S(2)}) %collective-permute-start) | collective-permute-done | bytes 516128 | tf_op jit(solution)/shard_map/ppermute | solution.py:15
  52.1 10.8 %collective-permute-done.2 = bf16[2,63,2048]{2,1,0:T(8,128)(2,1)} collective-permute-done((bf16[2,63,2048]{2,1,0:T(8,128)(2,1)}, bf16[2,63,2048]{2,1,0:T(8,128)(2,1)}, u32[]{:S(2)}, u32[]{:S(2)}) %collective-permute-start.2) | collective-permute-done | bytes 516128 | tf_op jit(solution)/shard_map/ppermute | solution.py:15
  65.3 14.2 %all-to-all-done.1 = bf16[16,128,896]{2,1,0:T(8,128)(2,1)} async-done(((bf16[16,128,896]{2,1,0:T(8,128)(2,1)}), bf16[16,128,896]{2,1,0:T(8,128)(2,1)}, u32[]{:S(2)}, u32[]{:S(2)}) %all-to-all-start.1) | async-done | bytes 3670048 | tf_op jit(solution)/shard_map/all_to_all | solution.py:43
  82.9 7.5 %convert_bitcast_fusion.3 = bf16[128,8,16,128]{3,1,2,0:T(8,128)(2,1)S(1)} fusion(bf16[1024,896]{1,0:T(8,128)(2,1)S(1)} %bitcast_select_fusion, bf16[896,2048]{1,0:T(8,128)(2,1)} %param.11), kind=kOutput, calls=%fused_computation.14 | convolution fusion | flops 3760193536 | bytes 9699328 | tf_op jit(solution)/shard_map/dot_general | solution.py:48
  92.4 4.7 %convert_bitcast_fusion.2 = bf16[128,8,16,128]{3,1,2,0:T(8,128)(2,1)S(1)} fusion(bf16[1024,896]{1,0:T(8,128)(2,1)S(1)} %bitcast_select_fusion, bf16[896,2048]{1,0:T(8,128)(2,1)S(1)} %copy-done.9), kind=kOutput, calls=%fused_computation.13 | convolution fusion | flops 3760193536 | bytes 9699328 | tf_op jit(solution)/shard_map/dot_general | solution.py:45
  111.1 7.9 %copy.70 = bf16[4,256,16,128]{3,2,1,0:T(8,128)(2,1)} copy(bf16[4,256,16,128]{1,3,2,0:T(8,128)(2,1)} %convert_bitcast_fusion.1) | data formatting | bytes 8388608 | tf_op jit(solution)/shard_map/convert_element_type | solution.py:84
  119.0 6.6 %bitcast_dynamic-update-slice_fusion.1 = bf16[1024,4096]{1,0:T(8,128)(2,1)} fusion(bf16[128,8,16,128]{3,2,1,0:T(8,128)(2,1)} %bitcast.84), kind=kLoop, calls=%fused_computation.7 | loop fusion | bytes 8388608
  125.6 8.4 %copy.72 = bf16[4,256,16,128]{3,2,1,0:T(8,128)(2,1)} copy(bf16[4,256,16,128]{1,3,2,0:T(8,128)(2,1)} %convert_bitcast_fusion) | data formatting | bytes 8388608 | tf_op jit(solution)/shard_map/convert_element_type | solution.py:88
  134.0 6.6 %bitcast_dynamic-update-slice_fusion = bf16[1024,4096]{1,0:T(8,128)(2,1)} fusion(bf16[1024,4096]{1,0:T(8,128)(2,1)} %bitcast_dynamic-update-slice_fusion.1, bf16[128,8,16,128]{3,2,1,0:T(8,128)(2,1)} %bitcast.83), kind=kLoop, calls=%fused_computation.6 | loop fusion | bytes 8388608 | tf_op jit(solution)/shard_map/concatenate | solution.py:89
  140.7 13.3 %fusion.49 = f32[896,4096]{1,0:T(8,128)} fusion(bf16[1024,896]{1,0:T(8,128)(2,1)S(1)} %copy-done.4, bf16[1024,4096]{1,0:T(8,128)(2,1)} %bitcast_dynamic-update-slice_fusion), kind=kOutput, calls=%fused_computation.75 | convolution fusion | flops 7516192768 | bytes 24903680 | tf_op jit(solution)/shard_map/px,pz->xz/dot_general | solution.py:122
  154.0 15.0 %fusion = f32[1024,896]{1,0:T(8,128)} fusion(bf16[1024,4096]{1,0:T(8,128)(2,1)} %bitcast_dynamic-update-slice_fusion, bf16[896,2048]{1,0:T(8,128)(2,1)} %param.11, bf16[896,2048]{1,0:T(8,128)(2,1)} %param.10), kind=kOutput, calls=%fused_computation.2 | convolution fusion | flops 7530872832 | bytes 19398656 | tf_op jit(solution)/shard_map/pz,xz->px/dot_general | solution.py:91
  169.0 4.7 %reshape.141 = f32[8,114688]{1,0:T(8,128)} reshape(f32[1024,896]{1,0:T(8,128)} %fusion) | data formatting | bytes 7340032 | tf_op jit(solution)/shard_map/reshape | solution.py:94
  173.7 8.0 %convolution_convert_fusion = bf16[16,128,896]{2,0,1:T(8,128)(2,1)S(1)} fusion(f32[128,896,8]{1,2,0:T(8,128)} %bitcast.85, s32[8]{0:T(128)S(1)} %get-tuple-element.26), kind=kOutput, calls=%fused_computation.29 | convolution fusion | flops 177996160 | bytes 7340064 | tf_op jit(solution)/shard_map/rs,rx->sx/dot_general | solution.py:95
  184.3 5.3 %all-to-all-start.2 = ((bf16[16,128,896]{2,1,0:T(8,128)(2,1)}), bf16[16,128,896]{2,1,0:T(8,128)(2,1)}, u32[]{:S(2)}, u32[]{:S(2)}) async-start(bf16[16,128,896]{2,1,0:T(8,128)(2,1)} %copy.73), calls=%async_computation.2 | async-start | bytes 7340032 | tf_op jit(solution)/shard_map/all_to_all | solution.py:98
  189.6 5.4 %fusion.23 = bf16[4,64,16,128]{3,1,2,0:T(8,128)(2,1)S(1)} fusion(bf16[4,256,16,128]{3,2,1,0:T(8,128)(2,1)} %bitcast.89, f32[4,16,64,256]{3,2,1,0:T(8,128)} %copy-done.1, f32[4,16,64]{2,1,0:T(8,128)S(1)} %get-tuple-element.29), kind=kOutput, calls=%fused_computation.33 | convolution fusion | flops 272105472 | bytes 9453568 | tf_op jit(solution)/shard_map/chqk,ckhd->cqhd/dot_general | solution.py:68
  216.1 12.7 %collective-permute-done.3 = bf16[2,63,2048]{2,1,0:T(8,128)(2,1)} collective-permute-done((bf16[2,63,2048]{2,1,0:T(8,128)(2,1)}, bf16[2,63,2048]{2,1,0:T(8,128)(2,1)}, u32[]{:S(2)}, u32[]{:S(2)}) %collective-permute-start.3) | collective-permute-done | bytes 516128 | tf_op jit(solution)/shard_map/ppermute | solution.py:15
  231.0 10.2 %all-to-all-done.2 = bf16[16,128,896]{2,1,0:T(8,128)(2,1)} async-done(((bf16[16,128,896]{2,1,0:T(8,128)(2,1)}), bf16[16,128,896]{2,1,0:T(8,128)(2,1)}, u32[]{:S(2)}, u32[]{:S(2)}) %all-to-all-start.2) | async-done | bytes 3670048 | tf_op jit(solution)/shard_map/all_to_all | solution.py:98
  241.2 4.4 %fusion.14 = f32[16,128,896]{2,0,1:T(8,128)S(1)} fusion(s32[16]{0:T(128)S(1)} %all_to_all.18, bf16[2,8,128,896]{3,2,1,0:T(8,128)(2,1)} %bitcast.41), kind=kOutput, calls=%fused_computation.25 | convolution fusion | flops 58720512 | bytes 11010112 | tf_op jit(solution)/shard_map/rs,sx->rx/dot_general | solution.py:108
  245.7 5.3 %copy.75 = f32[16,128,896]{2,1,0:T(8,128)} copy(f32[16,128,896]{2,0,1:T(8,128)S(1)} %fusion.14) | data formatting | bytes 14680064
  251.0 98.8 %all-reduce.3.cloned.1.call-done = f32[896,4096]{1,0:T(8,128)} async-done(((f32[896,4096]{1,0:T(8,128)}), f32[896,4096]{1,0:T(8,128)}) %all-reduce.3.cloned.1.call-update) | async-done | bytes 14680080
  (80 shorter events, 57.2 us)
Async XLA Ops:
  31.0 5.2 %copy-start.5 = (bf16[2,128,2048]{2,1,0:T(8,128)(2,1)S(1)}, bf16[2,128,2048]{2,1,0:T(8,128)(2,1)}, u32[]{:S(2)}) copy-start(bf16[2,128,2048]{2,1,0:T(8,128)(2,1)} %param.7) | copy-start | bytes 3145732
  31.0 6.6 %copy-start.6 = (bf16[2,128,2048]{2,1,0:T(8,128)(2,1)S(1)}, bf16[2,128,2048]{2,1,0:T(8,128)(2,1)}, u32[]{:S(2)}) copy-start(bf16[2,128,2048]{2,1,0:T(8,128)(2,1)} %param.8) | copy-start | bytes 3145732
  31.0 8.7 %copy-start.8 = (s32[1,1,4,2]{2,3,1,0:T(2,128)S(1)}, s32[1,1,4,2]{2,3,1,0:T(2,128)}, u32[]{:S(2)}) copy-start(s32[1,1,4,2]{2,3,1,0:T(2,128)} %param.12) | copy-start | bytes 100
  31.0 48.5 %all-to-all-start.1 = ((bf16[16,128,896]{2,1,0:T(8,128)(2,1)}), bf16[16,128,896]{2,1,0:T(8,128)(2,1)}, u32[]{:S(2)}, u32[]{:S(2)}) async-start(bf16[16,128,896]{2,1,0:T(8,128)(2,1)} %broadcast_select_fusion), calls=%async_computation.1 | async-start | bytes 7340032 | tf_op jit(solution)/shard_map/all_to_all | solution.py:43
  36.2 313.5 %all-reduce.3.cloned.1.call-start = ((), (), s32[]{:S(2)}) async-start(), calls=%async_computation.3 | async-start | bytes 29360128
  36.3 15.4 %collective-permute-start = (bf16[2,63,2048]{2,1,0:T(8,128)(2,1)S(1)}, bf16[2,63,2048]{2,1,0:T(8,128)(2,1)S(1)}, u32[]{:S(2)}, u32[]{:S(2)}) collective-permute-start(bf16[2,63,2048]{2,1,0:T(8,128)(2,1)S(1)} %slice.31), channel_id=1, source_target_pairs={{1,0},{2,1},{3,2},{4,3},{5,4},{6,5},{7,6},{8,7},{9,8},{10,9},{11,1... | collective-permute-start | bytes 1548296 | tf_op jit(solution)/shard_map/ppermute | solution.py:15
  38.4 24.5 %collective-permute-start.2 = (bf16[2,63,2048]{2,1,0:T(8,128)(2,1)}, bf16[2,63,2048]{2,1,0:T(8,128)(2,1)}, u32[]{:S(2)}, u32[]{:S(2)}) collective-permute-start(bf16[2,63,2048]{2,1,0:T(8,128)(2,1)} %slice.35), channel_id=1, source_target_pairs={{1,0},{2,1},{3,2},{4,3},{5,4},{6,5},{7,6},{8,7},{9,8},{10,9},{11,1... | collective-permute-start | bytes 1548296 | tf_op jit(solution)/shard_map/ppermute | solution.py:15
  82.9 8.9 %copy-start.3 = (bf16[1024,896]{1,0:T(8,128)(2,1)}, bf16[1024,896]{1,0:T(8,128)(2,1)S(1)}, u32[]{:S(2)}) copy-start(bf16[1024,896]{1,0:T(8,128)(2,1)S(1)} %bitcast_select_fusion) | copy-start | bytes 5505028
  90.4 2.0 copy-start.9
  92.4 11.3 %copy-start.2 = (bf16[128,8,16,128]{3,2,1,0:T(8,128)(2,1)}, bf16[128,8,16,128]{3,2,1,0:T(8,128)(2,1)S(1)}, u32[]{:S(2)}) copy-start(bf16[128,8,16,128]{3,2,1,0:T(8,128)(2,1)S(1)} %copy.79) | copy-start | bytes 12582916
  98.5 2.0 copy-start
  98.5 2.0 copy-start.7
  100.5 5.9 %copy-start.1 = (f32[4,16,64,256]{3,2,1,0:T(8,128)}, f32[4,16,64,256]{3,2,1,0:T(8,128)S(1)}, u32[]{:S(2)}) copy-start(f32[4,16,64,256]{3,2,1,0:T(8,128)S(1)} %get-tuple-element.30) | copy-start | bytes 12582916
  134.0 6.6 %copy-start.4 = (bf16[1024,896]{1,0:T(8,128)(2,1)S(1)}, bf16[1024,896]{1,0:T(8,128)(2,1)}, u32[]{:S(2)}) copy-start(bf16[1024,896]{1,0:T(8,128)(2,1)} %copy-done.3) | copy-start | bytes 5505028
  184.3 57.0 %all-to-all-start.2 = ((bf16[16,128,896]{2,1,0:T(8,128)(2,1)}), bf16[16,128,896]{2,1,0:T(8,128)(2,1)}, u32[]{:S(2)}, u32[]{:S(2)}) async-start(bf16[16,128,896]{2,1,0:T(8,128)(2,1)} %copy.73), calls=%async_computation.2 | async-start | bytes 7340032 | tf_op jit(solution)/shard_map/all_to_all | solution.py:98
  199.1 14.7 %collective-permute-start.1 = (bf16[2,63,2048]{2,1,0:T(8,128)(2,1)}, bf16[2,63,2048]{2,1,0:T(8,128)(2,1)}, u32[]{:S(2)}, u32[]{:S(2)}) collective-permute-start(bf16[2,63,2048]{2,1,0:T(8,128)(2,1)} %slice.44), channel_id=1, source_target_pairs={{0,1},{1,2},{2,3},{3,4},{4,5},{5,6},{6,7},{7,8},{8,9},{9,10},{10,1... | collective-permute-start | bytes 1548296 | tf_op jit(solution)/shard_map/ppermute | solution.py:15
  208.9 19.9 %collective-permute-start.3 = (bf16[2,63,2048]{2,1,0:T(8,128)(2,1)}, bf16[2,63,2048]{2,1,0:T(8,128)(2,1)}, u32[]{:S(2)}, u32[]{:S(2)}) collective-permute-start(bf16[2,63,2048]{2,1,0:T(8,128)(2,1)} %slice.46), channel_id=1, source_target_pairs={{0,1},{1,2},{2,3},{3,4},{4,5},{5,6},{6,7},{7,8},{8,9},{9,10},{10,1... | collective-permute-start | bytes 1548296 | tf_op jit(solution)/shard_map/ppermute | solution.py:15
Sparse Core Ops, SparseCore 0:
  154.1 195.6 all-reduce.2
where the time goes:
time: 363 us; the launch traced here: 359 us
  waiting for transfers between devices  160 us (44%)
  matrix products  72.9 us (20%)
  local copies, waits for them, and re-layouts  66.7 us (18%)
  starting transfers between devices  20.3 us (6%)
  between operations  14.6 us (4%)
  other arithmetic  13.2 us (4%)
  blocking collectives  11.2 us (3%)
    unnamed x2, waiting for transfers between devices  98.8 us
    ppermute x4, waiting for transfers between devices, shifted(): return lax.ppermute(array, axis, pairs)  36.5 us
    unnamed x28, local copies, waits for them, and re-layouts  18.4 us
    dot_general x1, matrix products, local(): jnp.einsum('pz,xz->px', proj_grads, both_weights, preferred_element_type=...  15 us
    all_to_all x1, waiting for transfers between devices, local(): lax.all_to_all(outgoing, 'dp', split_axis=0, concat_axis=0, tiled=True)  14.2 us
    dot_general x1, matrix products, local(): jnp.einsum('px,pz->xz', neighbours, proj_grads, preferred_element_type=jn...  13.3 us
    all_to_all x1, blocking collectives, local(): lax.all_to_all(request, 'dp', split_axis=0, concat_axis=0, tiled=True)  11.2 us
    all_to_all x1, waiting for transfers between devices, local(): lax.all_to_all(slot_grads.reshape(slot_count, NB_LEN, ENC).astype(jnp.bfl...  10.2 us
  transfers between devices with their start and end apart: 7, of which 7 were waited for; matrix products, arithmetic and copies ran while one was open for 18% of the time, Pallas kernels for 0%

commit v1 on v0

v1 whole, which is shorter than its diff:
```python
import functools

import jax
import jax.numpy as jnp
from jax import lax
from jax.experimental import pallas as pl
from jax.experimental.pallas import tpu as pltpu
from jax.sharding import PartitionSpec as P

HD = 128
SPAN = 64
LAG = SPAN - 1
NB_LEN = 128
CAP = 2
PAD = 8
BF = jnp.bfloat16
F32 = jnp.float32
MESH = pl.DeviceIdType.MESH
VMEM_LIMIT = 60 * 2**20


def dims(n_dp, n_seq):
    side = int(round(n_seq**0.5))
    return n_dp // 2, side


def position():
    dp, seq = lax.axis_index("dp"), lax.axis_index("seq")
    return dp, seq, dp // 2, dp % 2


def toward(nz, rel):
    dp, seq, z, c = position()
    dz, dc = rel // 2, rel % 2
    return (lax.rem(z + dz, nz) * 2 + lax.rem(c + dc, 2), seq)


def back(nz, rel):
    dp, seq, z, c = position()
    dz, dc = rel // 2, rel % 2
    return (lax.rem(z + nz - dz, nz) * 2 + lax.rem(c + dc, 2), seq)


def along(side, first, step):
    dp, seq, z, c = position()
    y, x = seq // side, seq % side
    by_y = (1 - c) if first else c
    ny = lax.rem(y + step * by_y, side)
    nx = lax.rem(x + step * (1 - by_y), side)
    return (dp, ny * side + nx)


def greet(devices):
    barrier = pltpu.get_barrier_semaphore()
    for device in devices:
        pl.semaphore_signal(barrier, inc=1, device_id=device, device_id_type=MESH)
    pl.semaphore_wait(barrier, len(devices))


def remote(src, dst, send, recv, device):
    return pltpu.make_async_remote_copy(
        src_ref=src,
        dst_ref=dst,
        send_sem=send,
        recv_sem=recv,
        device_id=device,
        device_id_type=MESH,
    )


def far_first(nz):
    return sorted(range(2 * nz), key=lambda r: (-min(r // 2, nz - r // 2), r))


def fetch_kernel(
    nz, side,
    req, slot, db, q, g,
    near, arr_out, qs, gs,
    outb, inb, arr, arr_s, heads,
    rq_s, rq_r, ga_s, ga_r, hd_s, hd_r, loc,
):
    n_seq = side * side
    dp, seq, z, c = position()
    before = (dp, lax.rem(seq + n_seq - 1, n_seq))
    after = (dp, lax.rem(seq + 1, n_seq))
    rels = [r for r in far_first(nz) if r]
    greet([toward(nz, r) for r in rels] + [before, after])
    asks = []
    for r in rels:
        copy = remote(req.at[r], arr.at[r], rq_s.at[r], rq_r.at[r], back(nz, r))
        copy.start()
        asks.append(copy)
    arr[0] = req[0]
    head_copies = []
    for t, ref in enumerate((q, g)):
        copy = remote(ref.at[:, 0:SPAN], heads.at[t], hd_s.at[t], hd_r.at[t], before)
        copy.start()
        head_copies.append(copy)
    for copy in asks:
        copy.wait_recv()
    to_smem = pltpu.make_async_copy(arr, arr_s, loc)
    to_smem.start()
    to_smem.wait()
    last_row = db.shape[0] - 1
    sends = []
    for r in rels:
        for k in range(CAP):
            row = jnp.clip(arr_s[r, 0, k], 0, last_row)
            outb[CAP * r + k] = db[row]
        part = pl.ds(CAP * r, CAP)
        copy = remote(outb.at[part], inb.at[part], ga_s.at[r], ga_r.at[r], toward(nz, r))
        copy.start()
        sends.append(copy)
    for k in range(CAP):
        row = jnp.clip(arr_s[0, 0, k], 0, last_row)
        inb[k] = db[row]
    arr_out[...] = arr[...]
    at_end = seq == n_seq - 1
    width = 256
    rows = q.shape[1]
    for t, (ref, out) in enumerate(((q, qs), (g, gs))):
        head_copies[t].wait_recv()
        for j in range(ref.shape[0]):

            def shift(i, carry, ref=ref, out=out, t=t, j=j):
                lanes = pl.ds(pl.multiple_of(i * width, width), width)
                own = ref[j, :, lanes].astype(F32)
                head = heads[t, j, :, lanes].astype(F32)
                head = jnp.where(at_end, jnp.zeros_like(head), head)
                both = jnp.concatenate([own, head], axis=0)
                moved = pltpu.roll(both, rows + SPAN - LAG, 0)[:rows].astype(BF)
                for u in range(rows // SPAN):
                    out[j * (rows // SPAN) + u, :, lanes] = moved[u * SPAN : (u + 1) * SPAN]
                return carry

            lax.fori_loop(0, ref.shape[2] // width, shift, 0)
    for copy in sends:
        copy.wait_recv()
    for i in range(near.shape[0]):
        near[i] = inb[slot[i]]
    for copy in asks + head_copies + sends:
        copy.wait_send()


def nt(a, b):
    return lax.dot_general(a, b, (((1,), (1,)), ((), ())), preferred_element_type=F32)


def tn(a, b):
    return lax.dot_general(a, b, (((0,), (0,)), ((), ())), preferred_element_type=F32)


def nn(a, b):
    return jnp.dot(a, b, preferred_element_type=F32)


def work_kernel(
    nz, side,
    inv, near, qs, gs, kw, vw,
    context, query_grad, returned, wgrad,
    retb, ctx, dq, tails, k2, v2, pg, ng, ngb, near_t, s0, s1, r0, r1, s2, r2, s3, r3,
    own_sem, rt_s, rt_r, tl_s, tl_r, p0_s, p0_r, p1_s, p1_r, p2_s, p2_r, p3_s, p3_r,
):
    n_seq = side * side
    dp, seq, z, c = position()
    y, x = seq // side, seq % side
    before = (dp, lax.rem(seq + n_seq - 1, n_seq))
    after = (dp, lax.rem(seq + 1, n_seq))
    rels = [r for r in far_first(nz) if r]
    steps = range(1, side)
    greet(
        [toward(nz, r) for r in rels]
        + [along(side, True, s) for s in steps]
        + [along(side, False, s) for s in steps]
        + [before, after]
    )
    blocks = qs.shape[0]
    refs = near.shape[0] // NB_LEN
    keys = near.shape[0] // blocks
    enc = near.shape[1]
    pairs = kw.shape[1] // (2 * HD)
    scale = HD**-0.5
    wide = 2 * HD
    first_head = lax.broadcasted_iota(jnp.int32, (SPAN, wide), 1) < HD

    def diagonal(a):
        zero = jnp.zeros_like(a)
        return jnp.concatenate(
            [jnp.where(first_head, a, zero), jnp.where(first_head, zero, a)], axis=0
        )

    def folded(a):
        return jnp.where(first_head, a[:SPAN], a[SPAN:]).astype(BF)

    ng[...] = jnp.zeros_like(ng)

    def pair(hp, carry):
        lanes = pl.ds(pl.multiple_of(hp * wide, wide), wide)
        k_lanes = pl.ds(pl.multiple_of(hp * 2 * wide, 2 * wide), wide)
        v_lanes = pl.ds(pl.multiple_of(hp * 2 * wide + wide, wide), wide)
        k2[...] = nn(near[...], kw[:, lanes]).astype(BF)
        v2[...] = nn(near[...], vw[:, lanes]).astype(BF)
        for b in range(blocks):
            part = slice(b * keys, (b + 1) * keys)
            kb, vb = k2[part], v2[part]
            qd, gd = diagonal(qs[b, :, lanes]), diagonal(gs[b, :, lanes])
            e = jnp.exp(nt(qd, kb) * scale)
            p = e / jnp.sum(e, axis=1, keepdims=True)
            half = p.astype(BF)
            pgr = nt(gd, vb)
            delta = jnp.sum(p * pgr, axis=1, keepdims=True)
            ds = (scale * p * (pgr - delta)).astype(BF)
            ctx[b, :, lanes] = folded(nn(half, vb))
            dq[b, :, lanes] = folded(nn(ds, kb))
            pg[part, k_lanes] = tn(ds, qd).astype(BF)
            pg[part, v_lanes] = tn(half, gd).astype(BF)
        ng[...] += nt(pg[:, k_lanes], kw[:, lanes]) + nt(pg[:, v_lanes], vw[:, lanes])
        return carry

    lax.fori_loop(0, pairs, pair, 0)
    waits = []
    for i in range(refs):
        ngb[i] = ng[i * NB_LEN : (i + 1) * NB_LEN].astype(BF)
    return_copies = []
    for r in rels:
        for k in range(CAP):
            retb[CAP * r + k] = ngb[inv[CAP * r + k]]
        part = pl.ds(CAP * r, CAP)
        copy = remote(retb.at[part], returned.at[part], rt_s.at[r], rt_r.at[r], back(nz, r))
        copy.start()
        return_copies.append(copy)
    for k in range(CAP):
        retb[k] = ngb[inv[k]]
    own_copy = pltpu.make_async_copy(retb.at[pl.ds(0, CAP)], returned.at[pl.ds(0, CAP)], own_sem)
    own_copy.start()
    tail_copies = []
    per_seq = blocks // tails.shape[1]
    for t, ref in enumerate((ctx, dq)):
        for j in range(tails.shape[1]):
            copy = remote(
                ref.at[per_seq * (j + 1) - 1], tails.at[t, j], tl_s.at[t, j], tl_r.at[t, j], after
            )
            copy.start()
            tail_copies.append(copy)
    half_rows = PAD * nz * n_seq
    rows_2 = PAD * nz
    rows_1 = rows_2 * side
    piece = min(128, half_rows)
    per_dev = enc // (2 * nz * n_seq)
    for a in range(2 * half_rows // piece):
        m = lax.broadcasted_iota(jnp.int32, (piece, enc), 0) + a * piece
        core, rest = m // half_rows, m % half_rows
        a1, a2, mz, row = rest // rows_1, (rest // rows_2) % side, (rest // PAD) % nz, rest % PAD
        cell = jnp.where(core == 0, a1 * side + a2, a2 * side + a1)
        column = ((mz * 2 + core) * n_seq + cell) * per_dev + row
        hit = (lax.broadcasted_iota(jnp.int32, (piece, enc), 1) == column) & (row < per_dev)
        pick = jnp.where(hit, 1.0, 0.0).astype(BF)
        near_t[a * piece : (a + 1) * piece] = nt(pick, near[...]).astype(BF)
    chunks = s0.shape[0]
    cw = s0.shape[3]
    sibling = (z * 2 + (1 - c), seq)
    my1 = jnp.where(c == 0, y, x)
    my2 = jnp.where(c == 0, x, y)
    phase0, phase1, phase2, phase3 = [], [], [], []

    def product(core, i):
        rows = pl.ds(pl.multiple_of(core * half_rows, half_rows), half_rows)
        out = nn(near_t[rows], pg[:, i * cw : (i + 1) * cw])
        return out.astype(BF).reshape(side, rows_1, cw)

    def send_first(i):
        phase0[i].wait_recv()
        s1[i] = (s1[i].astype(F32) + r0[i].astype(F32)).astype(BF)
        out = []
        for s in steps:
            to = lax.rem(my1 + s, side)
            copy = remote(
                s1.at[i, to], r1.at[i, s - 1], p1_s.at[i, s - 1], p1_r.at[i, s - 1],
                along(side, True, s),
            )
            copy.start()
            out.append(copy)
        phase1.append(out)

    for i in range(chunks):
        s0[i] = product(1 - c, i)
        copy = remote(s0.at[i], r0.at[i], p0_s.at[i], p0_r.at[i], sibling)
        copy.start()
        phase0.append(copy)
        s1[i] = product(c, i)
        if i:
            send_first(i - 1)
    send_first(chunks - 1)
    at_start = seq == 0
    width = 256
    rows = per_seq * SPAN
    for t, (ref, out) in enumerate(((ctx, context), (dq, query_grad))):
        for j in range(tails.shape[1]):
            tail_copies[t * tails.shape[1] + j].wait_recv()

            def shift(i, carry, ref=ref, out=out, t=t, j=j):
                lanes = pl.ds(pl.multiple_of(i * width, width), width)
                tail = tails[t, j, :, lanes].astype(F32)
                tail = jnp.where(at_start, jnp.zeros_like(tail), tail)
                own = [ref[per_seq * j + u, :, lanes].astype(F32) for u in range(per_seq)]
                both = jnp.concatenate([tail] + own, axis=0)
                out[j, :, lanes] = pltpu.roll(both, rows + LAG, 0)[:rows].astype(BF)
                return carry

            lax.fori_loop(0, ref.shape[2] // width, shift, 0)
    for i in range(chunks):
        total = s1[i, my1].astype(F32)
        for s in steps:
            phase1[i][s - 1].wait_recv()
            total = total + r1[i, s - 1].astype(F32)
        s2[i] = total.astype(BF).reshape(side, rows_2, cw)
        out = []
        for s in steps:
            to = lax.rem(my2 + s, side)
            copy = remote(
                s2.at[i, to], r2.at[i, s - 1], p2_s.at[i, s - 1], p2_r.at[i, s - 1],
                along(side, False, s),
            )
            copy.start()
            out.append(copy)
        phase2.append(out)
    for i in range(chunks):
        total = s2[i, my2].astype(F32)
        for s in steps:
            phase2[i][s - 1].wait_recv()
            total = total + r2[i, s - 1].astype(F32)
        keys_part = [total[:, a : a + wide] for a in range(0, cw, 2 * wide)]
        values_part = [total[:, a + wide : a + 2 * wide] for a in range(0, cw, 2 * wide)]
        for part in range(nz):
            row = slice(part * PAD, (part + 1) * PAD)
            for a in range(cw // (2 * wide)):
                both = jnp.concatenate([keys_part[a][row], values_part[a][row]], axis=0)
                at = i * cw // 2 + a * wide
                s3[part, :, at : at + wide] = both.astype(BF)
    for s in range(1, nz):
        copy = remote(
            s3.at[lax.rem(z + s, nz)], r3.at[s - 1], p3_s.at[s - 1], p3_r.at[s - 1],
            (lax.rem(z + s, nz) * 2 + c, seq),
        )
        copy.start()
        phase3.append(copy)
    total = s3[z].astype(F32)
    for s in range(1, nz):
        phase3[s - 1].wait_recv()
        total = total + r3[s - 1].astype(F32)
    wgrad[...] = total
    own_copy.wait()
    for copy in return_copies:
        copy.wait_recv()
    for copy in (
        return_copies + tail_copies + phase0 + sum(phase1, []) + sum(phase2, []) + phase3
    ):
        copy.wait_send()


def scatter_kernel(arrived, returned, out):
    out[...] = jnp.zeros_like(out)
    for s in range(returned.shape[0]):
        row = arrived[s]
        part = returned[s].astype(F32)
        out[jnp.maximum(row, 0)] += jnp.where(row >= 0, part, jnp.zeros_like(part))


def local(n_dp, n_seq, queries, d_context, database, key_weight, value_weight, shard, wanted):
    nz, side = dims(n_dp, n_seq)
    seqs, span, width = queries.shape
    blocks = seqs * span // SPAN
    refs = blocks * shard.shape[-1]
    slots = n_dp * CAP
    enc = database.shape[2]
    dp = lax.axis_index("dp")
    target, wanted = shard.reshape(refs), wanted.reshape(refs)
    order = jnp.arange(refs, dtype=jnp.int32)
    earlier = (target[:, None] == target[None, :]) & (order[None, :] < order[:, None])
    rank = jnp.sum(earlier.astype(jnp.int32), axis=1)
    rel = ((dp // 2 - target // 2 + nz) % nz) * 2 + (dp + target) % 2
    slot = rel * CAP + rank
    placed = slot[:, None] == jnp.arange(slots, dtype=jnp.int32)[None, :]
    request = jnp.sum(jnp.where(placed, wanted[:, None] + 1, 0), axis=0) - 1
    source = jnp.sum(jnp.where(placed, order[:, None], 0), axis=0)
    request = jnp.pad(request.reshape(n_dp, 1, CAP), ((0, 0), (0, 7), (0, 126)))
    vmem = pl.BlockSpec(memory_space=pltpu.VMEM)
    smem = pl.BlockSpec(memory_space=pltpu.SMEM)
    anywhere = pl.BlockSpec(memory_space=pl.ANY)
    dma = pltpu.SemaphoreType.DMA
    near, arrived, shifted_q, shifted_g = pl.pallas_call(
        functools.partial(fetch_kernel, nz, side),
        name="fetch",
        out_shape=(
            jax.ShapeDtypeStruct((refs, NB_LEN, enc), BF),
            jax.ShapeDtypeStruct((n_dp, 8, 128), jnp.int32),
            jax.ShapeDtypeStruct((blocks, SPAN, width), BF),
            jax.ShapeDtypeStruct((blocks, SPAN, width), BF),
        ),
        in_specs=[vmem, smem, vmem, vmem, vmem],
        out_specs=(vmem, vmem, vmem, vmem),
        scratch_shapes=[
            pltpu.VMEM((slots, NB_LEN, enc), BF),
            pltpu.VMEM((slots, NB_LEN, enc), BF),
            pltpu.VMEM((n_dp, 8, 128), jnp.int32),
            pltpu.SMEM((n_dp, 8, 128), jnp.int32),
            pltpu.VMEM((2, seqs, SPAN, width), BF),
            dma((n_dp,)),
            dma((n_dp,)),
            dma((n_dp,)),
            dma((n_dp,)),
            dma((2,)),
            dma((2,)),
            dma,
        ],
        compiler_params=pltpu.CompilerParams(
            collective_id=0, has_side_effects=True, vmem_limit_bytes=VMEM_LIMIT
        ),
    )(request, slot, database, queries, d_context)
    half_rows = PAD * nz * n_seq
    rows_2 = PAD * nz
    rows_1 = rows_2 * side
    chunk = 4 * 2 * HD
    chunks = 2 * width // chunk
    more = side - 1
    context, query_grad, returned, wgrad = pl.pallas_call(
        functools.partial(work_kernel, nz, side),
        name="work",
        out_shape=(
            jax.ShapeDtypeStruct((seqs, span, width), BF),
            jax.ShapeDtypeStruct((seqs, span, width), BF),
            jax.ShapeDtypeStruct((slots, NB_LEN, enc), BF),
            jax.ShapeDtypeStruct((2 * PAD, width), F32),
        ),
        in_specs=[smem, vmem, vmem, vmem, vmem, vmem],
        out_specs=(vmem, vmem, anywhere, vmem),
        scratch_shapes=[
            pltpu.VMEM((slots, NB_LEN, enc), BF),
            pltpu.VMEM((blocks, SPAN, width), BF),
            pltpu.VMEM((blocks, SPAN, width), BF),
            pltpu.VMEM((2, seqs, SPAN, width), BF),
            pltpu.VMEM((refs * NB_LEN, 2 * HD), BF),
            pltpu.VMEM((refs * NB_LEN, 2 * HD), BF),
            pltpu.VMEM((refs * NB_LEN, 2 * width), BF),
            pltpu.VMEM((refs * NB_LEN, enc), F32),
            pltpu.VMEM((refs, NB_LEN, enc), BF),
            pltpu.VMEM((2 * half_rows, refs * NB_LEN), BF),
            pltpu.VMEM((chunks, side, rows_1, chunk), BF),
            pltpu.VMEM((chunks, side, rows_1, chunk), BF),
            pltpu.VMEM((chunks, side, rows_1, chunk), BF),
            pltpu.VMEM((chunks, more, rows_1, chunk), BF),
            pltpu.VMEM((chunks, side, rows_2, chunk), BF),
            pltpu.VMEM((chunks, more, rows_2, chunk), BF),
            pltpu.VMEM((nz, 2 * PAD, width), BF),
            pltpu.VMEM((nz - 1, 2 * PAD, width), BF),
            dma,
            dma((n_dp,)),
            dma((n_dp,)),
            dma((2, seqs)),
            dma((2, seqs)),
            dma((chunks,)),
            dma((chunks,)),
            dma((chunks, more)),
            dma((chunks, more)),
            dma((chunks, more)),
            dma((chunks, more)),
            dma((nz - 1,)),
            dma((nz - 1,)),
        ],
        compiler_params=pltpu.CompilerParams(
            collective_id=1, has_side_effects=True, vmem_limit_bytes=VMEM_LIMIT
        ),
    )(
        source,
        near.reshape(refs * NB_LEN, enc),
        shifted_q,
        shifted_g,
        key_weight,
        value_weight,
    )
    rows = 16
    database_grad = pl.pallas_call(
        scatter_kernel,
        name="scatter",
        out_shape=jax.ShapeDtypeStruct(database.shape, F32),
        grid_spec=pltpu.PrefetchScalarGridSpec(
            num_scalar_prefetch=1,
            grid=(NB_LEN // rows,),
            in_specs=[pl.BlockSpec((slots, rows, enc), lambda i, s: (0, i, 0))],
            out_specs=pl.BlockSpec((database.shape[0], rows, enc), lambda i, s: (0, i, 0)),
        ),
    )(arrived[:, 0, :CAP].reshape(slots), returned)
    per_dev = enc // (n_dp * n_seq)
    return (
        context,
        query_grad,
        database_grad,
        wgrad[:per_dev],
        wgrad[PAD : PAD + per_dev],
    )


def solution(mesh):
    return jax.shard_map(
        functools.partial(local, mesh.shape["dp"], mesh.shape["seq"]),
        mesh=mesh,
        in_specs=(
            P("dp", "seq", None),
            P("dp", "seq", None),
            P(("dp", "seq"), None, None),
            P(),
            P(),
            P("dp", "seq", None, None),
            P("dp", "seq", None, None),
        ),
        out_specs=(
            P("dp", "seq", None),
            P("dp", "seq", None),
            P(("dp", "seq"), None, None),
            P(("dp", "seq"), None),
            P(("dp", "seq"), None),
        ),
        check_vma=False,
    )
```

time: 363 us -> 182 us (0.50); the launches traced: 359 us -> 182 us
  Pallas kernels: 0 us -> 173 us
  waiting for transfers between devices: 160 us -> 0 us
  matrix products: 72.9 us -> 0 us
  local copies, waits for them, and re-layouts: 66.7 us -> 6.58 us
  starting transfers between devices: 20.3 us -> 0 us
  between operations: 14.6 us -> 0.68 us
  other arithmetic: 13.2 us -> 1.49 us
  blocking collectives: 11.2 us -> 0 us
    pallas_call x0 -> x3, Pallas kernels: none -> 173 us  [the longest x1 105 us: local(): pl.pallas_call(functools.partial(work_kernel, nz, side), name='work', out...]
    unnamed x2 -> x0, waiting for transfers between devices: 98.8 us -> none
    dot_general x12 -> x0, matrix products: 72.9 us -> none  [the longest x1 15 us: local(): jnp.einsum('pz,xz->px', proj_grads, both_weights, preferred_element_type=...]
    ppermute x4 -> x0, waiting for transfers between devices: 36.5 us -> none  [shifted(): return lax.ppermute(array, axis, pairs)]
    all_to_all x2 -> x0, waiting for transfers between devices: 24.4 us -> none  [the longest x1 14.2 us: local(): lax.all_to_all(outgoing, 'dp', split_axis=0, concat_axis=0, tiled=True)]
    convert_element_type x5 -> x0, local copies, waits for them, and re-layouts: 21.3 us -> none  [the longest x1 8.4 us: local(): value_grads.astype(jnp.bfloat16).reshape(ref_count * NB_LEN, feat_width)]
    unnamed x28 -> x9, local copies, waits for them, and re-layouts: 18.4 us -> 2.72 us
    all_to_all x1 -> x0, blocking collectives: 11.2 us -> none  [local(): lax.all_to_all(request, 'dp', split_axis=0, concat_axis=0, tiled=True)]
  transfers between devices with their start and end apart: 7 -> 0, of which waited for: 7 -> 0; matrix products, arithmetic and copies ran while one was open for 18% -> 0% of each run, Pallas kernels for 0% -> 0%
where the time goes in v1:
time: 182 us
  Pallas kernels  173 us (95%)
  local copies, waits for them, and re-layouts  6.58 us (4%)
    pallas_call x1, Pallas kernels, local(): pl.pallas_call(functools.partial(work_kernel, nz, side), name='work', out...  105 us
    pallas_call x1, Pallas kernels, local(): pl.pallas_call(functools.partial(fetch_kernel, nz, side), name='fetch', o...  59.1 us
    pallas_call x1, Pallas kernels, local(): pl.pallas_call(scatter_kernel, name='scatter', out_shape=jax.ShapeDtypeSt...  8.26 us

profile of v1, /device:TPU:1, one launch (start us, length us, event | category | flops | bytes accessed | tf_op | source)
XLA Modules:
  0.0 181.6 jit_solution(485233862359638593)
XLA Ops:
  0.6 0.7 broadcast_add_fusion
  1.3 0.1 copy.19
  1.4 0.1 add.81
  1.5 0.8 copy.18
  2.3 0.1 reshape.102
  2.4 0.2 convert_reduce_fusion
  2.6 0.0 copy-start.2
  2.6 0.6 select_reduce_fusion
  3.2 0.1 sub.28
  3.3 0.6 pad.4.req
  3.9 0.0 copy-done.2
  3.9 59.1 %fetch.1 = (bf16[8,128,896]{2,1,0:T(8,128)(2,1)}, s32[8,8,128]{2,1,0:T(8,128)}, bf16[4,64,2048]{2,1,0:T(8,128)(2,1)}, bf16[4,64,2048]{2,1,0:T(8,128)(2,1)}) custom-call(s32[8,8,128]{2,1,0:T(8,128)} %pad.4.req, s32[8]{0:T(128)} %copy-done.2, bf16[16,128,896]{2,1,0:T(8,128)(2,1)} %db.1, bf16[2,128,2048]{2,1,0:T(8,128)(2,1)} %q.1, bf16[2,128,2048]{2,1,0:T(8,128)(2,1)} %g.1), custom_call_target="tpu_custom_call" | custom-call | tf_op jit(solution)/shard_map/fetch/pallas_call | solution.py:391
  63.0 0.8 slice_reduce_fusion
  63.8 0.6 reshape_squeeze.3.arrived
  64.4 105.5 %work.1 = (bf16[2,128,2048]{2,1,0:T(8,128)(2,1)}, bf16[2,128,2048]{2,1,0:T(8,128)(2,1)}, bf16[16,128,896]{2,1,0:T(8,128)(2,1)}, f32[16,2048]{1,0:T(8,128)}) custom-call(s32[16]{0:T(128)} %get-tuple-element.22.inv, bf16[1024,896]{1,0:T(8,128)(2,1)} %bitcast.2, bf16[4,64,2048]{2,1,0:T(8,128)(2,1)} %get-tuple-element.14.qs, ...), custom_call_target="tpu_custom_call" | custom-call | tf_op jit(solution)/shard_map/work/pallas_call | solution.py:426
  169.9 1.5 fusion.5
  171.4 0.0 copy-start.1
  171.4 0.0 copy-start
  171.4 8.3 %scatter.1 = f32[16,128,896]{2,1,0:T(8,128)} custom-call(s32[16]{0:T(128)} %reshape_squeeze.3.arrived, bf16[16,128,896]{2,1,0:T(8,128)(2,1)} %get-tuple-element.19.returned), custom_call_target="tpu_custom_call" | custom-call | tf_op jit(solution)/shard_map/scatter/pallas_call | solution.py:482
  179.7 0.0 copy-done.1
  179.7 1.0 copy.23
  180.6 0.0 copy-done
  180.6 1.0 copy.24
  (2 shorter events, 0.0 us)
Async XLA Ops:
  2.6 1.3 copy-start.2
  171.4 8.3 %copy-start.1 = (bf16[2,128,2048]{2,1,0:T(8,128)(2,1)S(1)}, bf16[2,128,2048]{2,1,0:T(8,128)(2,1)}, u32[]{:S(2)}) copy-start(bf16[2,128,2048]{2,1,0:T(8,128)(2,1)} %get-tuple-element.30) | copy-start | bytes 3145732
  171.4 9.2 %copy-start = (bf16[2,128,2048]{2,1,0:T(8,128)(2,1)S(1)}, bf16[2,128,2048]{2,1,0:T(8,128)(2,1)}, u32[]{:S(2)}) copy-start(bf16[2,128,2048]{2,1,0:T(8,128)(2,1)} %get-tuple-element.31) | copy-start | bytes 3145732

commit v2 on v1

v2 whole, which is shorter than its diff:
```python
import functools

import jax
import jax.numpy as jnp
from jax import lax
from jax.experimental import pallas as pl
from jax.experimental.pallas import tpu as pltpu
from jax.sharding import PartitionSpec as P

HD = 128
SPAN = 64
LAG = SPAN - 1
NB_LEN = 128
CAP = 2
PAD = 8
BF = jnp.bfloat16
F32 = jnp.float32
MESH = pl.DeviceIdType.MESH
VMEM_LIMIT = 62 * 2**20


def dims(n_dp, n_seq):
    side = int(round(n_seq**0.5))
    return n_dp // 2, side


def position():
    dp, seq = lax.axis_index("dp"), lax.axis_index("seq")
    return dp, seq, dp // 2, dp % 2


def toward(nz, rel):
    dp, seq, z, c = position()
    dz, dc = rel // 2, rel % 2
    return (lax.rem(z + dz, nz) * 2 + lax.rem(c + dc, 2), seq)


def back(nz, rel):
    dp, seq, z, c = position()
    dz, dc = rel // 2, rel % 2
    return (lax.rem(z + nz - dz, nz) * 2 + lax.rem(c + dc, 2), seq)


def along(side, first, step):
    dp, seq, z, c = position()
    y, x = seq // side, seq % side
    by_y = (1 - c) if first else c
    ny = lax.rem(y + step * by_y, side)
    nx = lax.rem(x + step * (1 - by_y), side)
    return (dp, ny * side + nx)


def greet(devices):
    barrier = pltpu.get_barrier_semaphore()
    for device in devices:
        pl.semaphore_signal(barrier, inc=1, device_id=device, device_id_type=MESH)
    pl.semaphore_wait(barrier, len(devices))


def remote(src, dst, send, recv, device):
    return pltpu.make_async_remote_copy(
        src_ref=src,
        dst_ref=dst,
        send_sem=send,
        recv_sem=recv,
        device_id=device,
        device_id_type=MESH,
    )


def far_first(nz):
    return sorted(range(2 * nz), key=lambda r: (-min(r // 2, nz - r // 2), r))


def nt(a, b):
    return lax.dot_general(a, b, (((1,), (1,)), ((), ())), preferred_element_type=F32)


def tn(a, b):
    return lax.dot_general(a, b, (((0,), (0,)), ((), ())), preferred_element_type=F32)


def nn(a, b):
    return jnp.dot(a, b, preferred_element_type=F32)


def main_kernel(
    nz, side,
    named, db_hbm, q_hbm, g_hbm, kw_hbm, vw_hbm,
    context, query_grad, returned, arrived, wgrad,
    db, outb, inb, req, arr, arr_s, heads, q, g, qs, gs, kw, vw, kv, pg, ng, sa_k, sa_v, sb_k, sb_v, tails,
    r2, s3, r3,
    ld, rq_s, rq_r, ga_s, ga_r, hd_s, hd_r, own_sem, rt_s, rt_r, tl_s, tl_r,
    p0_s, p0_r, p1_s, p1_r, p2_s, p2_r, p3_s, p3_r, free0, free1,
):
    n_seq = side * side
    dp, seq, z, c = position()
    y, x = seq // side, seq % side
    before = (dp, lax.rem(seq + n_seq - 1, n_seq))
    after = (dp, lax.rem(seq + 1, n_seq))
    sibling = (z * 2 + (1 - c), seq)
    rels = [r for r in far_first(nz) if r]
    steps = range(1, side)
    loads = []
    pairs_in = ((db_hbm, db), (kw_hbm, kw), (vw_hbm, vw), (q_hbm, q), (g_hbm, g))
    for i, (src, dst) in enumerate(pairs_in):
        copy = pltpu.make_async_copy(src, dst, ld.at[i])
        copy.start()
        loads.append(copy)
    picks, blocks = named.shape[2], named.shape[3]
    refs = blocks * picks
    slots = CAP * 2 * nz
    held = db_hbm.shape[0]
    both = [named[0, 0, i % picks, i // picks] for i in range(refs)]
    target, row_of = [a // held for a in both], [a % held for a in both]
    slot = []
    for i in range(refs):
        rank = sum([jnp.where(target[j] == target[i], 1, 0) for j in range(i)], jnp.int32(0))
        dz = lax.rem(z + nz - target[i] // 2, nz)
        dc = lax.rem(c + target[i], 2)
        slot.append((dz * 2 + dc) * CAP + jnp.minimum(rank, CAP - 1))
    lane = lax.broadcasted_iota(jnp.int32, (8, 128), 1)
    source = []
    for r in range(2 * nz):
        tile = jnp.zeros((8, 128), jnp.int32)
        for k in range(CAP):
            here = [slot[i] == CAP * r + k for i in range(refs)]
            asked = sum([jnp.where(here[i], row_of[i] + 1, 0) for i in range(refs)], jnp.int32(0))
            mine = sum([jnp.where(here[i], i, 0) for i in range(refs)], jnp.int32(0))
            source.append(jnp.minimum(mine, refs - 1))
            tile = jnp.where(lane == k, asked - 1, tile)
        req[r] = tile
    greet(
        [toward(nz, r) for r in rels]
        + [along(side, True, s) for s in steps]
        + [along(side, False, s) for s in steps]
        + [before, after]
    )
    asks = []
    for r in rels:
        copy = remote(req.at[r], arr.at[r], rq_s.at[r], rq_r.at[r], back(nz, r))
        copy.start()
        asks.append(copy)
    arr[0] = req[0]
    head_copies = []
    for t, ref in enumerate((q_hbm, g_hbm)):
        copy = remote(ref.at[:, 0:SPAN], heads.at[t], hd_s.at[t], hd_r.at[t], before)
        copy.start()
        head_copies.append(copy)
    for copy in asks:
        copy.wait_recv()
    to_smem = pltpu.make_async_copy(arr, arr_s, ld.at[5])
    to_smem.start()
    loads[0].wait()
    to_smem.wait()
    last_row = db.shape[0] - 1
    sends = {}
    for r in rels:
        for k in range(CAP):
            row = jnp.clip(arr_s[r, 0, k], 0, last_row)
            outb[CAP * r + k] = db[row]
        part = pl.ds(CAP * r, CAP)
        copy = remote(outb.at[part], inb.at[part], ga_s.at[r], ga_r.at[r], toward(nz, r))
        copy.start()
        sends[r] = copy
    for k in range(CAP):
        row = jnp.clip(arr_s[0, 0, k], 0, last_row)
        inb[k] = db[row]
    for r in range(2 * nz):
        for k in range(CAP):
            arrived[CAP * r + k] = arr_s[r, 0, k]
    enc = db.shape[2]
    half_rows = PAD * nz * n_seq
    rows_2 = PAD * nz
    rows_1 = rows_2 * side
    piece = NB_LEN
    per_dev = enc // (2 * nz * n_seq)
    pieces = 2 * half_rows // piece
    for a in range(pieces):
        m = lax.broadcasted_iota(jnp.int32, (piece, 128), 0) + a * piece
        core, rest = m // half_rows, m % half_rows
        a1, a2, mz, row = rest // rows_1, (rest // rows_2) % side, (rest // PAD) % nz, rest % PAD
        cell = jnp.where(core == 0, a1 * side + a2, a2 * side + a1)
        column = ((mz * 2 + core) * n_seq + cell) * per_dev + row
        column = jnp.where(row < per_dev, column, enc)
        for o in range(0, enc, 128):
            hit = lax.broadcasted_iota(jnp.int32, (piece, 128), 1) + o == column
            db[a, :, o : o + 128] = jnp.where(hit, 1.0, 0.0).astype(BF)
    at_end = seq == n_seq - 1
    width = 256
    seqs, rows = q.shape[0], q.shape[1]
    per_seq = rows // SPAN
    for t, (ref, out) in enumerate(((q, qs), (g, gs))):
        loads[3 + t].wait()
        head_copies[t].wait_recv()
        for j in range(seqs):

            def shift(i, carry, ref=ref, out=out, t=t, j=j):
                lanes = pl.ds(pl.multiple_of(i * width, width), width)
                own = ref[j, :, lanes].astype(F32)
                head = heads[t, j, :, lanes].astype(F32)
                head = jnp.where(at_end, jnp.zeros_like(head), head)
                both = jnp.concatenate([own, head], axis=0)
                moved = pltpu.roll(both, rows + SPAN - LAG, 0)[:rows].astype(BF)
                for u in range(per_seq):
                    out[j * per_seq + u, :, lanes] = moved[u * SPAN : (u + 1) * SPAN]
                return carry

            lax.fori_loop(0, ref.shape[2] // width, shift, 0)
    hw = kw.shape[1]
    loads[1].wait()
    loads[2].wait()
    step_lanes = 512
    for r in [0, 1] + [r for r in rels if r != 1]:
        if r:
            sends[r].wait_recv()

        def project(i, carry, r=r):
            lanes = pl.ds(pl.multiple_of(i * step_lanes, step_lanes), step_lanes)
            later = pl.ds(pl.multiple_of(hw + i * step_lanes, step_lanes), step_lanes)
            rows_in = inb[CAP * r : CAP * (r + 1)].reshape(CAP * NB_LEN, enc)
            keys = nn(rows_in, kw[:, lanes]).astype(BF)
            kv[CAP * r : CAP * (r + 1), :, lanes] = keys.reshape(CAP, NB_LEN, step_lanes)
            values = nn(rows_in, vw[:, lanes]).astype(BF)
            kv[CAP * r : CAP * (r + 1), :, later] = values.reshape(CAP, NB_LEN, step_lanes)
            return carry

        lax.fori_loop(0, hw // step_lanes, project, 0)
    scale = HD**-0.5
    wide = 2 * HD
    first_head = lax.broadcasted_iota(jnp.int32, (SPAN, wide), 1) < HD

    def diagonal(a):
        zero = jnp.zeros_like(a)
        return jnp.concatenate(
            [jnp.where(first_head, a, zero), jnp.where(first_head, zero, a)], axis=0
        )

    def folded(a):
        return jnp.where(first_head, a[:SPAN], a[SPAN:]).astype(BF)

    def attend(hp, stage_k, stage_v, beside):
        lanes = pl.ds(pl.multiple_of(hp * wide, wide), wide)
        later = pl.ds(pl.multiple_of(hw + hp * wide, wide), wide)
        every = range(blocks)
        kb, vb, qd, gd = [], [], [], []
        for b in every:
            mine = [slot[picks * b + i] for i in range(picks)]
            kb.append(jnp.concatenate([kv[i, :, lanes] for i in mine], axis=0))
            vb.append(jnp.concatenate([kv[i, :, later] for i in mine], axis=0))
            qd.append(diagonal(qs[b, :, lanes]))
            gd.append(diagonal(gs[b, :, lanes]))
        scores = [nt(qd[b], kb[b]) for b in every]
        pgr = [nt(gd[b], vb[b]) for b in every]
        beside(0)
        p = []
        for b in every:
            e = jnp.exp(scores[b] * scale)
            p.append(e / jnp.sum(e, axis=1, keepdims=True))
        half = [p[b].astype(BF) for b in every]
        beside(1)
        out = [folded(nn(half[b], vb[b])) for b in every]
        value_g = [tn(half[b], gd[b]).astype(BF) for b in every]
        beside(2)
        ds = []
        for b in every:
            delta = jnp.sum(p[b] * pgr[b], axis=1, keepdims=True)
            ds.append((scale * p[b] * (pgr[b] - delta)).astype(BF))
        beside(3)
        back_out = [folded(nn(ds[b], kb[b])) for b in every]
        key_g = [tn(ds[b], qd[b]).astype(BF) for b in every]
        for b in every:
            rows_b = slice(b * picks * NB_LEN, (b + 1) * picks * NB_LEN)
            qs[b, :, lanes] = out[b]
            gs[b, :, lanes] = back_out[b]
            stage_k[rows_b] = key_g[b]
            stage_v[rows_b] = value_g[b]
            pg[picks * b : picks * (b + 1), :, lanes] = key_g[b].reshape(picks, NB_LEN, wide)
            pg[picks * b : picks * (b + 1), :, later] = value_g[b].reshape(picks, NB_LEN, wide)

    def add_near(hp, stage_k, stage_v):
        lanes = pl.ds(pl.multiple_of(hp * wide, wide), wide)

        def add(b):
            rows_b = slice(b * picks * NB_LEN, (b + 1) * picks * NB_LEN)
            ng[rows_b] += nt(stage_k[rows_b], kw[:, lanes]) + nt(stage_v[rows_b], vw[:, lanes])

        return add

    ng[...] = jnp.zeros_like(ng)
    sb_k[...] = jnp.zeros_like(sb_k)
    sb_v[...] = jnp.zeros_like(sb_v)

    def two_pairs(i, carry):
        attend(2 * i, sa_k, sa_v, add_near(jnp.maximum(2 * i - 1, 0), sb_k, sb_v))
        attend(2 * i + 1, sb_k, sb_v, add_near(2 * i, sa_k, sa_v))
        return carry

    lax.fori_loop(0, hw // (2 * wide), two_pairs, 0)
    last = add_near(hw // wide - 1, sb_k, sb_v)
    for b in range(blocks):
        last(b)
    for i in range(refs):
        db[pieces + i] = ng[i * NB_LEN : (i + 1) * NB_LEN].astype(BF)
    pl.semaphore_signal(free0, inc=1, device_id=sibling, device_id_type=MESH)
    for s in steps:
        pl.semaphore_signal(free1, inc=1, device_id=along(side, True, s), device_id_type=MESH)
    for copy in sends.values():
        copy.wait_send()
    return_copies = []

    def give_back(r):
        for k in range(CAP):
            outb[CAP * r + k] = db[pieces + source[CAP * r + k]]
        part = pl.ds(CAP * r, CAP)
        if r:
            copy = remote(outb.at[part], returned.at[part], rt_s.at[r], rt_r.at[r], back(nz, r))
            return_copies.append(copy)
        else:
            copy = pltpu.make_async_copy(outb.at[part], returned.at[part], own_sem)
            own_copies.append(copy)
        copy.start()

    own_copies = []
    chunks = p0_s.shape[0]
    cw = 2 * hw // chunks
    my1 = jnp.where(c == 0, y, x)
    my2 = jnp.where(c == 0, x, y)
    phase0, phase1, phase2, phase3 = [], [], [], []

    def rows_of(a):
        return pl.ds(pl.multiple_of(a * rows_2, rows_2), rows_2)

    def lanes_of(a):
        return pl.ds(pl.multiple_of(a * cw, cw), cw)

    def product(core, i, base):
        start = pl.multiple_of(core * half_rows, half_rows)
        some = jnp.concatenate([part[pl.ds(start, half_rows)] for part in near_t], axis=1)
        for o in range(0, cw, step_lanes):
            these = pg[:, :, i * cw + o : i * cw + o + step_lanes]
            out = nn(some, these.reshape(refs * NB_LEN, step_lanes)).astype(BF)
            for a in range(side):
                kv[base + i, :, a * cw + o : a * cw + o + step_lanes] = out[
                    a * rows_1 : (a + 1) * rows_1
                ]

    def multiply(i):
        product(1 - c, i, 0)
        if i == 0:
            pl.semaphore_wait(free0, 1)
        copy = remote(kv.at[i], kv.at[2 * chunks + i], p0_s.at[i], p0_r.at[i], sibling)
        copy.start()
        phase0.append(copy)
        product(c, i, chunks)

    def send_first(i):
        phase0[i].wait_recv()
        kv[chunks + i] = (kv[chunks + i].astype(F32) + kv[2 * chunks + i].astype(F32)).astype(BF)
        if i == 0:
            pl.semaphore_wait(free1, side - 1)
        out = []
        for s in steps:
            to = lax.rem(my1 + s, side)
            copy = remote(
                kv.at[chunks + i, :, lanes_of(to)],
                kv.at[3 * chunks + i, :, pl.ds((s - 1) * cw, cw)],
                p1_s.at[i, s - 1], p1_r.at[i, s - 1], along(side, True, s),
            )
            copy.start()
            out.append(copy)
        phase1.append(out)

    for r in rels + [0]:
        give_back(r)
    tail_copies = []
    for t, ref in enumerate((qs, gs)):
        for j in range(seqs):
            copy = remote(
                ref.at[per_seq * (j + 1) - 1], tails.at[t, j], tl_s.at[t, j], tl_r.at[t, j], after
            )
            copy.start()
            tail_copies.append(copy)
    near_t = (sa_k, sa_v, sb_k, sb_v)
    for i in range(0, refs, 2):
        both = jnp.concatenate([inb[slot[i]], inb[slot[i + 1]]], axis=0)
        near_t[i // 2][...] = nt(db[0:pieces].reshape(2 * half_rows, enc), both).astype(BF)
    for i in range(chunks + 1):
        if i < chunks:
            multiply(i)
        if i:
            send_first(i - 1)
    at_start = seq == 0
    outs = []
    for t, (ref, out, hbm) in enumerate(((qs, q, context), (gs, g, query_grad))):
        for j in range(seqs):
            tail_copies[t * seqs + j].wait_recv()

            def unshift(i, carry, ref=ref, out=out, t=t, j=j):
                lanes = pl.ds(pl.multiple_of(i * width, width), width)
                tail = tails[t, j, :, lanes].astype(F32)
                tail = jnp.where(at_start, jnp.zeros_like(tail), tail)
                own = [ref[per_seq * j + u, :, lanes].astype(F32) for u in range(per_seq)]
                both = jnp.concatenate([tail] + own, axis=0)
                out[j, :, lanes] = pltpu.roll(both, rows + LAG, 0)[:rows].astype(BF)
                return carry

            lax.fori_loop(0, ref.shape[2] // width, unshift, 0)
        copy = pltpu.make_async_copy(out, hbm, ld.at[6 + t])
        copy.start()
        outs.append(copy)
    for i in range(chunks):
        total = kv[chunks + i, :, lanes_of(my1)].astype(F32)
        for s in steps:
            phase1[i][s - 1].wait_recv()
            total = total + kv[3 * chunks + i, :, (s - 1) * cw : s * cw].astype(F32)
        kv[3 * chunks + i, :, (side - 1) * cw : side * cw] = total.astype(BF)
        out = []
        for s in steps:
            to = lax.rem(my2 + s, side)
            copy = remote(
                kv.at[3 * chunks + i, rows_of(to), pl.ds((side - 1) * cw, cw)], r2.at[i, s - 1], p2_s.at[i, s - 1], p2_r.at[i, s - 1],
                along(side, False, s),
            )
            copy.start()
            out.append(copy)
        phase2.append(out)
    totals = []
    for i in range(chunks):
        total = kv[3 * chunks + i, rows_of(my2), (side - 1) * cw : side * cw].astype(F32)
        for s in steps:
            phase2[i][s - 1].wait_recv()
            total = total + r2[i, s - 1].astype(F32)
        totals.append(total)
        if i >= chunks // 2:
            a = i - chunks // 2
            for part in range(nz):
                row = slice(part * PAD, (part + 1) * PAD)
                both = jnp.concatenate([totals[a][row], total[row]], axis=0)
                s3[part, :, a * cw : (a + 1) * cw] = both.astype(BF)
    for s in range(1, nz):
        copy = remote(
            s3.at[lax.rem(z + s, nz)], r3.at[s - 1], p3_s.at[s - 1], p3_r.at[s - 1],
            (lax.rem(z + s, nz) * 2 + c, seq),
        )
        copy.start()
        phase3.append(copy)
    total = s3[z].astype(F32)
    for s in range(1, nz):
        phase3[s - 1].wait_recv()
        total = total + r3[s - 1].astype(F32)
    wgrad[...] = total
    for copy in outs + own_copies:
        copy.wait()
    for copy in return_copies:
        copy.wait_recv()
    for copy in (
        asks + head_copies + return_copies + tail_copies + phase0
        + sum(phase1, []) + sum(phase2, []) + phase3
    ):
        copy.wait_send()


def finish_kernel(arrived, returned, wgrad, out, key_part, value_part):
    @pl.when(pl.program_id(0) == 0)
    def _():
        per_dev = key_part.shape[0]
        key_part[...] = wgrad[0:per_dev]
        value_part[...] = wgrad[PAD : PAD + per_dev]

    out[...] = jnp.zeros_like(out)
    for s in range(returned.shape[0]):
        row = arrived[s]
        part = returned[s].astype(F32)
        out[jnp.clip(row, 0, out.shape[0] - 1)] += jnp.where(row >= 0, part, jnp.zeros_like(part))


def local(n_dp, n_seq, queries, d_context, database, key_weight, value_weight, shard, wanted):
    nz, side = dims(n_dp, n_seq)
    seqs, span, width = queries.shape
    blocks = seqs * span // SPAN
    refs = blocks * shard.shape[-1]
    slots = n_dp * CAP
    enc = database.shape[2]
    vmem = pl.BlockSpec(memory_space=pltpu.VMEM)
    smem = pl.BlockSpec(memory_space=pltpu.SMEM)
    anywhere = pl.BlockSpec(memory_space=pl.ANY)
    dma = pltpu.SemaphoreType.DMA
    regular = pltpu.SemaphoreType.REGULAR
    rows_2 = PAD * nz
    chunks = 4
    chunk = 2 * width // chunks
    more = side - 1
    context, query_grad, returned, arrived, wgrad = pl.pallas_call(
        functools.partial(main_kernel, nz, side),
        name="main",
        out_shape=(
            jax.ShapeDtypeStruct((seqs, span, width), BF),
            jax.ShapeDtypeStruct((seqs, span, width), BF),
            jax.ShapeDtypeStruct((slots, NB_LEN, enc), BF),
            jax.ShapeDtypeStruct((slots,), jnp.int32),
            jax.ShapeDtypeStruct((2 * PAD, width), F32),
        ),
        in_specs=[smem] + [anywhere] * 5,
        out_specs=(anywhere, anywhere, anywhere, smem, vmem),
        scratch_shapes=[
            pltpu.VMEM((database.shape[0], NB_LEN, enc), BF),
            pltpu.VMEM((slots, NB_LEN, enc), BF),
            pltpu.VMEM((slots, NB_LEN, enc), BF),
            pltpu.VMEM((n_dp, 8, 128), jnp.int32),
            pltpu.VMEM((n_dp, 8, 128), jnp.int32),
            pltpu.SMEM((n_dp, 8, 128), jnp.int32),
            pltpu.VMEM((2, seqs, SPAN, width), BF),
            pltpu.VMEM((seqs, span, width), BF),
            pltpu.VMEM((seqs, span, width), BF),
            pltpu.VMEM((blocks, SPAN, width), BF),
            pltpu.VMEM((blocks, SPAN, width), BF),
            pltpu.VMEM((enc, width), BF),
            pltpu.VMEM((enc, width), BF),
            pltpu.VMEM((slots, NB_LEN, 2 * width), BF),
            pltpu.VMEM((refs, NB_LEN, 2 * width), BF),
            pltpu.VMEM((refs * NB_LEN, enc), F32),
            pltpu.VMEM((refs * NB_LEN, 2 * HD), BF),
            pltpu.VMEM((refs * NB_LEN, 2 * HD), BF),
            pltpu.VMEM((refs * NB_LEN, 2 * HD), BF),
            pltpu.VMEM((refs * NB_LEN, 2 * HD), BF),
            pltpu.VMEM((2, seqs, SPAN, width), BF),
            pltpu.VMEM((chunks, more, rows_2, chunk), BF),
            pltpu.VMEM((nz, 2 * PAD, width), BF),
            pltpu.VMEM((nz - 1, 2 * PAD, width), BF),
            dma((8,)),
            dma((n_dp,)),
            dma((n_dp,)),
            dma((n_dp,)),
            dma((n_dp,)),
            dma((2,)),
            dma((2,)),
            dma,
            dma((n_dp,)),
            dma((n_dp,)),
            dma((2, seqs)),
            dma((2, seqs)),
            dma((chunks,)),
            dma((chunks,)),
            dma((chunks, more)),
            dma((chunks, more)),
            dma((chunks, more)),
            dma((chunks, more)),
            dma((nz - 1,)),
            dma((nz - 1,)),
            regular,
            regular,
        ],
        compiler_params=pltpu.CompilerParams(
            collective_id=0, has_side_effects=True, vmem_limit_bytes=VMEM_LIMIT
        ),
    )((shard * database.shape[0] + wanted).swapaxes(2, 3), database, queries, d_context, key_weight, value_weight)
    rows = 32
    per_dev = enc // (n_dp * n_seq)
    part = jax.ShapeDtypeStruct((per_dev, width), F32)
    database_grad, key_part, value_part = pl.pallas_call(
        finish_kernel,
        name="finish",
        out_shape=(jax.ShapeDtypeStruct(database.shape, F32), part, part),
        grid_spec=pltpu.PrefetchScalarGridSpec(
            num_scalar_prefetch=1,
            grid=(NB_LEN // rows,),
            in_specs=[
                pl.BlockSpec((slots, rows, enc), lambda i, s: (0, i, 0)),
                pl.BlockSpec((2 * PAD, width), lambda i, s: (0, 0)),
            ],
            out_specs=(
                pl.BlockSpec((database.shape[0], rows, enc), lambda i, s: (0, i, 0)),
                pl.BlockSpec((per_dev, width), lambda i, s: (0, 0)),
                pl.BlockSpec((per_dev, width), lambda i, s: (0, 0)),
            ),
        ),
        compiler_params=pltpu.CompilerParams(vmem_limit_bytes=VMEM_LIMIT),
    )(arrived, returned, wgrad)
    return context, query_grad, database_grad, key_part, value_part


def solution(mesh):
    return jax.shard_map(
        functools.partial(local, mesh.shape["dp"], mesh.shape["seq"]),
        mesh=mesh,
        in_specs=(
            P("dp", "seq", None),
            P("dp", "seq", None),
            P(("dp", "seq"), None, None),
            P(),
            P(),
            P("dp", "seq", None, None),
            P("dp", "seq", None, None),
        ),
        out_specs=(
            P("dp", "seq", None),
            P("dp", "seq", None),
            P(("dp", "seq"), None, None),
            P(("dp", "seq"), None),
            P(("dp", "seq"), None),
        ),
        check_vma=False,
    )
```

time: 182 us -> 157 us (0.86)
  Pallas kernels: 173 us -> 152 us
  local copies, waits for them, and re-layouts: 6.58 us -> 3.28 us
    pallas_call x3 -> x2, Pallas kernels: 173 us -> 152 us  [the longest x1 145 us: local(): pl.pallas_call(functools.partial(main_kernel, nz, side), name='main', out...]
    slice x2 -> x0, local copies, waits for them, and re-layouts: 2.3 us -> none  [the longest x1 1.53 us: local(): wgrad[PAD:PAD + per_dev]]
where the time goes in v2:
time: 157 us
  Pallas kernels  152 us (97%)
  local copies, waits for them, and re-layouts  3.28 us (2%)
    pallas_call x1, Pallas kernels, local(): pl.pallas_call(functools.partial(main_kernel, nz, side), name='main', out...  145 us
    pallas_call x1, Pallas kernels, local(): pl.pallas_call(finish_kernel, name='finish', out_shape=(jax.ShapeDtypeStr...  6.78 us
    unnamed x4, local copies, waits for them, and re-layouts  3.28 us

profile of v2, /device:TPU:1, one launch (start us, length us, event | category | flops | bytes accessed | tf_op | source)
XLA Modules:
  0.0 157.1 jit_solution(17364825526171865198)
XLA Ops:
  0.6 1.3 add_bitcast_fusion.named
  1.9 145.2 %main.1 = (bf16[2,128,2048]{2,1,0:T(8,128)(2,1)}, bf16[2,128,2048]{2,1,0:T(8,128)(2,1)}, bf16[16,128,896]{2,1,0:T(8,128)(2,1)}, s32[16]{0:T(128)}, f32[16,2048]{1,0:T(8,128)}) custom-call(s32[1,1,2,4]{3,2,1,0:T(2,128)} %add_bitcast_fusion.named, bf16[16,128,896]{2,1,0:T(8,128)(2,1)} %db_hbm.1, bf16[2,128,2048]{2,1,0:T(8,128)(2,1)} %q_hbm.1, ...), custom_call_target="tpu_custom_call" | custom-call | tf_op jit(solution)/shard_map/main/pallas_call | solution.py:494
  147.1 0.0 copy-start
  147.1 6.8 %finish.1 = (f32[16,128,896]{2,1,0:T(8,128)}, f32[7,2048]{1,0:T(8,128)}, f32[7,2048]{1,0:T(8,128)}) custom-call(s32[16]{0:T(128)} %get-tuple-element.15.arrived, bf16[16,128,896]{2,1,0:T(8,128)(2,1)} %get-tuple-element.16.returned, f32[16,2048]{1,0:T(8,128)} %get-tuple-element.17.wgrad), custom_call_target="tpu_custom_call" | custom-call | tf_op jit(solution)/shard_map/finish/pallas_call | solution.py:561
  153.8 2.3 %copy.14 = bf16[2,128,2048]{2,1,0:T(8,128)(2,1)} copy(bf16[2,128,2048]{2,1,0:T(8,128)(2,1)} %get-tuple-element.26) | data formatting | bytes 2097152
  156.2 0.0 copy-done
  156.2 1.0 copy.15
Async XLA Ops:
  147.1 9.1 %copy-start = (bf16[2,128,2048]{2,1,0:T(8,128)(2,1)S(1)}, bf16[2,128,2048]{2,1,0:T(8,128)(2,1)}, u32[]{:S(2)}) copy-start(bf16[2,128,2048]{2,1,0:T(8,128)(2,1)} %get-tuple-element.27) | copy-start | bytes 3145732

commit v3 on v2

--- a/solution.py
+++ b/solution.py
@@ -87,7 +87,7 @@
 def main_kernel(
     nz, side,
     named, db_hbm, q_hbm, g_hbm, kw_hbm, vw_hbm,
-    context, query_grad, returned, arrived, wgrad,
+    ctx_out, dq_out, tails_out, returned, arrived, wgrad,
     db, outb, inb, req, arr, arr_s, heads, q, g, qs, gs, kw, vw, kv, pg, ng, sa_k, sa_v, sb_k, sb_v, tails,
     r2, s3, r3,
     ld, rq_s, rq_r, ga_s, ga_r, hd_s, hd_r, own_sem, rt_s, rt_r, tl_s, tl_r,
@@ -169,6 +169,7 @@
     for r in range(2 * nz):
         for k in range(CAP):
             arrived[CAP * r + k] = arr_s[r, 0, k]
+    arrived[slots] = seq
     enc = db.shape[2]
     half_rows = PAD * nz * n_seq
     rows_2 = PAD * nz
@@ -291,9 +292,19 @@
     sb_k[...] = jnp.zeros_like(sb_k)
     sb_v[...] = jnp.zeros_like(sb_v)
 
+    def tail_copy(i, t, j):
+        lanes = pl.ds(pl.multiple_of(i * 2 * wide, 2 * wide), 2 * wide)
+        return remote(
+            (qs, gs)[t].at[per_seq * (j + 1) - 1, :, lanes], tails.at[t, j, :, lanes],
+            tl_s.at[i, t, j], tl_r.at[i, t, j], after,
+        )
+
     def two_pairs(i, carry):
         attend(2 * i, sa_k, sa_v, add_near(jnp.maximum(2 * i - 1, 0), sb_k, sb_v))
         attend(2 * i + 1, sb_k, sb_v, add_near(2 * i, sa_k, sa_v))
+        for t in range(2):
+            for j in range(seqs):
+                tail_copy(i, t, j).start()
         return carry
 
     lax.fori_loop(0, hw // (2 * wide), two_pairs, 0)
@@ -373,14 +384,11 @@
 
     for r in rels + [0]:
         give_back(r)
-    tail_copies = []
-    for t, ref in enumerate((qs, gs)):
-        for j in range(seqs):
-            copy = remote(
-                ref.at[per_seq * (j + 1) - 1], tails.at[t, j], tl_s.at[t, j], tl_r.at[t, j], after
-            )
-            copy.start()
-            tail_copies.append(copy)
+    outs = []
+    for t, (ref, hbm) in enumerate(((qs, ctx_out), (gs, dq_out))):
+        copy = pltpu.make_async_copy(ref, hbm, ld.at[6 + t])
+        copy.start()
+        outs.append(copy)
     near_t = (sa_k, sa_v, sb_k, sb_v)
     for i in range(0, refs, 2):
         both = jnp.concatenate([inb[slot[i]], inb[slot[i + 1]]], axis=0)
@@ -390,25 +398,17 @@
             multiply(i)
         if i:
             send_first(i - 1)
-    at_start = seq == 0
-    outs = []
-    for t, (ref, out, hbm) in enumerate(((qs, q, context), (gs, g, query_grad))):
-        for j in range(seqs):
-            tail_copies[t * seqs + j].wait_recv()
-
-            def unshift(i, carry, ref=ref, out=out, t=t, j=j):
-                lanes = pl.ds(pl.multiple_of(i * width, width), width)
-                tail = tails[t, j, :, lanes].astype(F32)
-                tail = jnp.where(at_start, jnp.zeros_like(tail), tail)
-                own = [ref[per_seq * j + u, :, lanes].astype(F32) for u in range(per_seq)]
-                both = jnp.concatenate([tail] + own, axis=0)
-                out[j, :, lanes] = pltpu.roll(both, rows + LAG, 0)[:rows].astype(BF)
-                return carry
-
-            lax.fori_loop(0, ref.shape[2] // width, unshift, 0)
-        copy = pltpu.make_async_copy(out, hbm, ld.at[6 + t])
-        copy.start()
-        outs.append(copy)
+    tail_copies = [
+        tail_copy(i, t, j)
+        for t in range(2)
+        for j in range(seqs)
+        for i in range(hw // (2 * wide))
+    ]
+    for copy in tail_copies:
+        copy.wait_recv()
+    copy = pltpu.make_async_copy(tails, tails_out, ld.at[8])
+    copy.start()
+    outs.append(copy)
     for i in range(chunks):
         total = kv[chunks + i, :, lanes_of(my1)].astype(F32)
         for s in steps:
@@ -461,15 +461,28 @@
         copy.wait_send()
 
 
-def finish_kernel(arrived, returned, wgrad, out, key_part, value_part):
+def finish_kernel(
+    arrived, returned, wgrad, ctx, dq, tails, out, key_part, value_part, context, query_grad
+):
     @pl.when(pl.program_id(0) == 0)
     def _():
         per_dev = key_part.shape[0]
         key_part[...] = wgrad[0:per_dev]
         value_part[...] = wgrad[PAD : PAD + per_dev]
 
+    slots, seqs = returned.shape[0], tails.shape[1]
+    per_seq = ctx.shape[0] // seqs
+    rows = per_seq * SPAN
+    at_start = arrived[slots] == 0
+    for t, (ref, here) in enumerate(((ctx, context), (dq, query_grad))):
+        for j in range(seqs):
+            tail = tails[t, j].astype(F32)
+            tail = jnp.where(at_start, jnp.zeros_like(tail), tail)
+            own = [ref[per_seq * j + u].astype(F32) for u in range(per_seq)]
+            both = jnp.concatenate([tail] + own, axis=0)
+            here[j] = pltpu.roll(both, rows + LAG, 0)[:rows].astype(BF)
     out[...] = jnp.zeros_like(out)
-    for s in range(returned.shape[0]):
+    for s in range(slots):
         row = arrived[s]
         part = returned[s].astype(F32)
         out[jnp.clip(row, 0, out.shape[0] - 1)] += jnp.where(row >= 0, part, jnp.zeros_like(part))
@@ -491,18 +504,19 @@
     chunks = 4
     chunk = 2 * width // chunks
     more = side - 1
-    context, query_grad, returned, arrived, wgrad = pl.pallas_call(
+    ctx, dq, tails, returned, arrived, wgrad = pl.pallas_call(
         functools.partial(main_kernel, nz, side),
         name="main",
         out_shape=(
-            jax.ShapeDtypeStruct((seqs, span, width), BF),
-            jax.ShapeDtypeStruct((seqs, span, width), BF),
+            jax.ShapeDtypeStruct((blocks, SPAN, width), BF),
+            jax.ShapeDtypeStruct((blocks, SPAN, width), BF),
+            jax.ShapeDtypeStruct((2, seqs, SPAN, width), BF),
             jax.ShapeDtypeStruct((slots, NB_LEN, enc), BF),
-            jax.ShapeDtypeStruct((slots,), jnp.int32),
+            jax.ShapeDtypeStruct((slots + 1,), jnp.int32),
             jax.ShapeDtypeStruct((2 * PAD, width), F32),
         ),
         in_specs=[smem] + [anywhere] * 5,
-        out_specs=(anywhere, anywhere, anywhere, smem, vmem),
+        out_specs=(anywhere, anywhere, anywhere, anywhere, smem, vmem),
         scratch_shapes=[
             pltpu.VMEM((database.shape[0], NB_LEN, enc), BF),
             pltpu.VMEM((slots, NB_LEN, enc), BF),
@@ -528,7 +542,7 @@
             pltpu.VMEM((chunks, more, rows_2, chunk), BF),
             pltpu.VMEM((nz, 2 * PAD, width), BF),
             pltpu.VMEM((nz - 1, 2 * PAD, width), BF),
-            dma((8,)),
+            dma((9,)),
             dma((n_dp,)),
             dma((n_dp,)),
             dma((n_dp,)),
@@ -538,8 +552,8 @@
             dma,
             dma((n_dp,)),
             dma((n_dp,)),
-            dma((2, seqs)),
-            dma((2, seqs)),
+            dma((width // (4 * HD), 2, seqs)),
+            dma((width // (4 * HD), 2, seqs)),
             dma((chunks,)),
             dma((chunks,)),
             dma((chunks, more)),
@@ -558,25 +572,33 @@
     rows = 32
     per_dev = enc // (n_dp * n_seq)
     part = jax.ShapeDtypeStruct((per_dev, width), F32)
-    database_grad, key_part, value_part = pl.pallas_call(
+    steps = NB_LEN // rows
+    lanes = width // steps
+    placed = jax.ShapeDtypeStruct(queries.shape, BF)
+    database_grad, key_part, value_part, context, query_grad = pl.pallas_call(
         finish_kernel,
         name="finish",
-        out_shape=(jax.ShapeDtypeStruct(database.shape, F32), part, part),
+        out_shape=(jax.ShapeDtypeStruct(database.shape, F32), part, part, placed, placed),
         grid_spec=pltpu.PrefetchScalarGridSpec(
             num_scalar_prefetch=1,
-            grid=(NB_LEN // rows,),
+            grid=(steps,),
             in_specs=[
                 pl.BlockSpec((slots, rows, enc), lambda i, s: (0, i, 0)),
                 pl.BlockSpec((2 * PAD, width), lambda i, s: (0, 0)),
+                pl.BlockSpec((blocks, SPAN, lanes), lambda i, s: (0, 0, i)),
+                pl.BlockSpec((blocks, SPAN, lanes), lambda i, s: (0, 0, i)),
+                pl.BlockSpec((2, seqs, SPAN, lanes), lambda i, s: (0, 0, 0, i)),
             ],
             out_specs=(
                 pl.BlockSpec((database.shape[0], rows, enc), lambda i, s: (0, i, 0)),
                 pl.BlockSpec((per_dev, width), lambda i, s: (0, 0)),
                 pl.BlockSpec((per_dev, width), lambda i, s: (0, 0)),
+                pl.BlockSpec((seqs, span, lanes), lambda i, s: (0, 0, i)),
+                pl.BlockSpec((seqs, span, lanes), lambda i, s: (0, 0, i)),
             ),
         ),
         compiler_params=pltpu.CompilerParams(vmem_limit_bytes=VMEM_LIMIT),
-    )(arrived, returned, wgrad)
+    )(arrived, returned, wgrad, ctx, dq, tails)
     return context, query_grad, database_grad, key_part, value_part
 
 

time: 157 us -> 141 us (0.90)
  Pallas kernels: 152 us -> 138 us
  local copies, waits for them, and re-layouts: 3.28 us -> 0 us
    pallas_call x1, Pallas kernels: 145 us -> 130 us  [local(): pl.pallas_call(functools.partial(main_kernel, nz, side), name='main', out...]
    unnamed x4 -> x0, local copies, waits for them, and re-layouts: 3.28 us -> none
where the time goes in v3:
time: 141 us; the launch traced here: 140 us
  Pallas kernels  138 us (98%)
    pallas_call x1, Pallas kernels, local(): pl.pallas_call(functools.partial(main_kernel, nz, side), name='main', out...  130 us
    pallas_call x1, Pallas kernels, local(): pl.pallas_call(finish_kernel, name='finish', out_shape=(jax.ShapeDtypeStr...  8.24 us

profile of v3, /device:TPU:1, one launch (start us, length us, event | category | flops | bytes accessed | tf_op | source)
XLA Modules:
  0.0 140.3 jit_solution(5733052513118537266)
XLA Ops:
  0.6 1.3 add_bitcast_fusion.named
  1.9 130.0 %main.1 = (bf16[4,64,2048]{2,1,0:T(8,128)(2,1)}, bf16[4,64,2048]{2,1,0:T(8,128)(2,1)}, bf16[2,2,64,2048]{3,2,1,0:T(8,128)(2,1)}, bf16[16,128,896]{2,1,0:T(8,128)(2,1)}, s32[17]{0:T(128)}, /*index=5*/f32[16,2048]{1,0:T(8,128)}) custom-call(s32[1,1,2,4]{3,2,1,0:T(2,128)} %add_bitcast_fusion.named, bf16[16,128,896]{2,1,0:T(8,128)(2,1)} %db_hbm.1, ...), custom_call_target="tpu_custom_call" | custom-call | tf_op jit(solution)/shard_map/main/pallas_call | solution.py:507
  131.9 8.2 %finish.1 = (f32[16,128,896]{2,1,0:T(8,128)}, f32[7,2048]{1,0:T(8,128)}, f32[7,2048]{1,0:T(8,128)}, bf16[2,128,2048]{2,1,0:T(8,128)(2,1)}, bf16[2,128,2048]{2,1,0:T(8,128)(2,1)}) custom-call(s32[17]{0:T(128)} %get-tuple-element.16.arrived, bf16[16,128,896]{2,1,0:T(8,128)(2,1)} %get-tuple-element.17.returned, f32[16,2048]{1,0:T(8,128)} %get-tuple-element.18.wgrad, ...), custom_call_target="tpu_custom_call" | custom-call | tf_op jit(solution)/shard_map/finish/pallas_call | solution.py:578

commit v4 on v3

--- a/solution.py
+++ b/solution.py
@@ -86,7 +86,7 @@
 
 def main_kernel(
     nz, side,
-    named, db_hbm, q_hbm, g_hbm, kw_hbm, vw_hbm,
+    shard, wanted, db_hbm, q_hbm, g_hbm, kw_hbm, vw_hbm,
     ctx_out, dq_out, tails_out, returned, arrived, wgrad,
     db, outb, inb, req, arr, arr_s, heads, q, g, qs, gs, kw, vw, kv, pg, ng, sa_k, sa_v, sb_k, sb_v, tails,
     r2, s3, r3,
@@ -107,27 +107,41 @@
         copy = pltpu.make_async_copy(src, dst, ld.at[i])
         copy.start()
         loads.append(copy)
-    picks, blocks = named.shape[2], named.shape[3]
+    picks, blocks = shard.shape[2], shard.shape[3]
     refs = blocks * picks
-    slots = CAP * 2 * nz
-    held = db_hbm.shape[0]
-    both = [named[0, 0, i % picks, i // picks] for i in range(refs)]
-    target, row_of = [a // held for a in both], [a % held for a in both]
+    near_by = 2 * nz
+    slots = CAP * near_by
+    named = [[shard[0, 0, i, b] for i in range(picks)] for b in range(blocks)]
+    order = [jnp.int32(b) for b in range(blocks)]
+    for e0 in reversed(range(blocks)):
+        for e1 in reversed(range(e0 + 1, blocks)):
+            apart = 0
+            for i in named[e0]:
+                for j in named[e1]:
+                    apart = apart + jnp.where(i == j, 1, 0)
+            wish = [e0, e1] + [b for b in range(blocks) if b not in (e0, e1)]
+            order = [jnp.where(apart == 0, w, o) for w, o in zip(wish, order)]
+    place = [
+        sum([jnp.where(order[n] == b, n, 0) for n in range(blocks)], jnp.int32(0))
+        for b in range(blocks)
+    ]
+    target = [shard[0, 0, i % picks, order[i // picks]] for i in range(refs)]
+    row_of = [wanted[0, 0, i % picks, order[i // picks]] for i in range(refs)]
     slot = []
     for i in range(refs):
         rank = sum([jnp.where(target[j] == target[i], 1, 0) for j in range(i)], jnp.int32(0))
         dz = lax.rem(z + nz - target[i] // 2, nz)
         dc = lax.rem(c + target[i], 2)
-        slot.append((dz * 2 + dc) * CAP + jnp.minimum(rank, CAP - 1))
+        slot.append(jnp.minimum(rank, CAP - 1) * near_by + dz * 2 + dc)
     lane = lax.broadcasted_iota(jnp.int32, (8, 128), 1)
-    source = []
+    source = {}
     for r in range(2 * nz):
         tile = jnp.zeros((8, 128), jnp.int32)
         for k in range(CAP):
-            here = [slot[i] == CAP * r + k for i in range(refs)]
+            here = [slot[i] == k * near_by + r for i in range(refs)]
             asked = sum([jnp.where(here[i], row_of[i] + 1, 0) for i in range(refs)], jnp.int32(0))
             mine = sum([jnp.where(here[i], i, 0) for i in range(refs)], jnp.int32(0))
-            source.append(jnp.minimum(mine, refs - 1))
+            source[k, r] = jnp.minimum(mine, refs - 1)
             tile = jnp.where(lane == k, asked - 1, tile)
         req[r] = tile
     greet(
@@ -155,21 +169,26 @@
     to_smem.wait()
     last_row = db.shape[0] - 1
     sends = {}
-    for r in rels:
-        for k in range(CAP):
+    first_sent = [1] + [r for r in rels if r != 1]
+    for k in range(CAP):
+        for r in first_sent:
+            here = k * near_by + r
             row = jnp.clip(arr_s[r, 0, k], 0, last_row)
-            outb[CAP * r + k] = db[row]
-        part = pl.ds(CAP * r, CAP)
-        copy = remote(outb.at[part], inb.at[part], ga_s.at[r], ga_r.at[r], toward(nz, r))
-        copy.start()
-        sends[r] = copy
+            outb[here] = db[row]
+            copy = remote(
+                outb.at[here], inb.at[here], ga_s.at[k, r], ga_r.at[k, r], toward(nz, r)
+            )
+            copy.start()
+            sends[k, r] = copy
     for k in range(CAP):
         row = jnp.clip(arr_s[0, 0, k], 0, last_row)
-        inb[k] = db[row]
-    for r in range(2 * nz):
+        inb[k * near_by] = db[row]
+    for r in range(near_by):
         for k in range(CAP):
-            arrived[CAP * r + k] = arr_s[r, 0, k]
+            arrived[k * near_by + r] = arr_s[r, 0, k]
     arrived[slots] = seq
+    for b in range(blocks):
+        arrived[slots + 1 + b] = place[b]
     enc = db.shape[2]
     half_rows = PAD * nz * n_seq
     rows_2 = PAD * nz
@@ -191,20 +210,24 @@
     width = 256
     seqs, rows = q.shape[0], q.shape[1]
     per_seq = rows // SPAN
-    for t, (ref, out) in enumerate(((q, qs), (g, gs))):
+    for t in range(2):
         loads[3 + t].wait()
         head_copies[t].wait_recv()
-        for j in range(seqs):
-
-            def shift(i, carry, ref=ref, out=out, t=t, j=j):
+    for t, (ref, out) in enumerate(((q, qs), (g, gs))):
+        for n in range(blocks):
+
+            def shift(i, carry, ref=ref, out=out, t=t, n=n):
                 lanes = pl.ds(pl.multiple_of(i * width, width), width)
+                j, u = order[n] // per_seq, order[n] % per_seq
                 own = ref[j, :, lanes].astype(F32)
                 head = heads[t, j, :, lanes].astype(F32)
                 head = jnp.where(at_end, jnp.zeros_like(head), head)
                 both = jnp.concatenate([own, head], axis=0)
-                moved = pltpu.roll(both, rows + SPAN - LAG, 0)[:rows].astype(BF)
-                for u in range(per_seq):
-                    out[j * per_seq + u, :, lanes] = moved[u * SPAN : (u + 1) * SPAN]
+                moved = pltpu.roll(both, rows + SPAN - LAG, 0)
+                chosen = moved[:SPAN]
+                for v in range(1, per_seq):
+                    chosen = jnp.where(u == v, moved[v * SPAN : (v + 1) * SPAN], chosen)
+                out[n, :, lanes] = chosen.astype(BF)
                 return carry
 
             lax.fori_loop(0, ref.shape[2] // width, shift, 0)
@@ -212,21 +235,27 @@
     loads[1].wait()
     loads[2].wait()
     step_lanes = 512
-    for r in [0, 1] + [r for r in rels if r != 1]:
-        if r:
-            sends[r].wait_recv()
-
-        def project(i, carry, r=r):
-            lanes = pl.ds(pl.multiple_of(i * step_lanes, step_lanes), step_lanes)
-            later = pl.ds(pl.multiple_of(hw + i * step_lanes, step_lanes), step_lanes)
-            rows_in = inb[CAP * r : CAP * (r + 1)].reshape(CAP * NB_LEN, enc)
-            keys = nn(rows_in, kw[:, lanes]).astype(BF)
-            kv[CAP * r : CAP * (r + 1), :, lanes] = keys.reshape(CAP, NB_LEN, step_lanes)
-            values = nn(rows_in, vw[:, lanes]).astype(BF)
-            kv[CAP * r : CAP * (r + 1), :, later] = values.reshape(CAP, NB_LEN, step_lanes)
-            return carry
-
-        lax.fori_loop(0, hw // step_lanes, project, 0)
+
+    def arrive(k):
+        for m in [0] + sorted(range(1, nz), key=lambda m: (-min(m, nz - m), m)):
+            for r in (2 * m, 2 * m + 1):
+                if r:
+                    sends[k, r].wait_recv()
+            first = k * near_by + 2 * m
+            pair_of = slice(first, first + 2)
+
+            def project(i, carry, pair_of=pair_of):
+                lanes = pl.ds(pl.multiple_of(i * step_lanes, step_lanes), step_lanes)
+                later = pl.ds(pl.multiple_of(hw + i * step_lanes, step_lanes), step_lanes)
+                rows_in = inb[pair_of].reshape(2 * NB_LEN, enc)
+                keys = nn(rows_in, kw[:, lanes]).astype(BF)
+                kv[pair_of, :, lanes] = keys.reshape(2, NB_LEN, step_lanes)
+                values = nn(rows_in, vw[:, lanes]).astype(BF)
+                kv[pair_of, :, later] = values.reshape(2, NB_LEN, step_lanes)
+                return carry
+
+            lax.fori_loop(0, hw // step_lanes, project, 0)
+
     scale = HD**-0.5
     wide = 2 * HD
     first_head = lax.broadcasted_iota(jnp.int32, (SPAN, wide), 1) < HD
@@ -240,36 +269,35 @@
     def folded(a):
         return jnp.where(first_head, a[:SPAN], a[SPAN:]).astype(BF)
 
-    def attend(hp, stage_k, stage_v, beside):
+    def attend(every, hp, stage_k, stage_v, beside):
         lanes = pl.ds(pl.multiple_of(hp * wide, wide), wide)
         later = pl.ds(pl.multiple_of(hw + hp * wide, wide), wide)
-        every = range(blocks)
-        kb, vb, qd, gd = [], [], [], []
+        kb, vb, qd, gd = {}, {}, {}, {}
         for b in every:
             mine = [slot[picks * b + i] for i in range(picks)]
-            kb.append(jnp.concatenate([kv[i, :, lanes] for i in mine], axis=0))
-            vb.append(jnp.concatenate([kv[i, :, later] for i in mine], axis=0))
-            qd.append(diagonal(qs[b, :, lanes]))
-            gd.append(diagonal(gs[b, :, lanes]))
-        scores = [nt(qd[b], kb[b]) for b in every]
-        pgr = [nt(gd[b], vb[b]) for b in every]
+            kb[b] = jnp.concatenate([kv[i, :, lanes] for i in mine], axis=0)
+            vb[b] = jnp.concatenate([kv[i, :, later] for i in mine], axis=0)
+            qd[b] = diagonal(qs[b, :, lanes])
+            gd[b] = diagonal(gs[b, :, lanes])
+        scores = {b: nt(qd[b], kb[b]) for b in every}
+        pgr = {b: nt(gd[b], vb[b]) for b in every}
         beside(0)
-        p = []
+        p = {}
         for b in every:
             e = jnp.exp(scores[b] * scale)
-            p.append(e / jnp.sum(e, axis=1, keepdims=True))
-        half = [p[b].astype(BF) for b in every]
+            p[b] = e / jnp.sum(e, axis=1, keepdims=True)
+        half = {b: p[b].astype(BF) for b in every}
         beside(1)
-        out = [folded(nn(half[b], vb[b])) for b in every]
-        value_g = [tn(half[b], gd[b]).astype(BF) for b in every]
+        out = {b: folded(nn(half[b], vb[b])) for b in every}
+        value_g = {b: tn(half[b], gd[b]).astype(BF) for b in every}
         beside(2)
-        ds = []
+        ds = {}
         for b in every:
             delta = jnp.sum(p[b] * pgr[b], axis=1, keepdims=True)
-            ds.append((scale * p[b] * (pgr[b] - delta)).astype(BF))
+            ds[b] = (scale * p[b] * (pgr[b] - delta)).astype(BF)
         beside(3)
-        back_out = [folded(nn(ds[b], kb[b])) for b in every]
-        key_g = [tn(ds[b], qd[b]).astype(BF) for b in every]
+        back_out = {b: folded(nn(ds[b], kb[b])) for b in every}
+        key_g = {b: tn(ds[b], qd[b]).astype(BF) for b in every}
         for b in every:
             rows_b = slice(b * picks * NB_LEN, (b + 1) * picks * NB_LEN)
             qs[b, :, lanes] = out[b]
@@ -279,10 +307,13 @@
             pg[picks * b : picks * (b + 1), :, lanes] = key_g[b].reshape(picks, NB_LEN, wide)
             pg[picks * b : picks * (b + 1), :, later] = value_g[b].reshape(picks, NB_LEN, wide)
 
-    def add_near(hp, stage_k, stage_v):
+    def add_near(every, hp, stage_k, stage_v):
         lanes = pl.ds(pl.multiple_of(hp * wide, wide), wide)
 
-        def add(b):
+        def add(step):
+            if step % 2 or step // 2 >= len(every):
+                return
+            b = every[step // 2]
             rows_b = slice(b * picks * NB_LEN, (b + 1) * picks * NB_LEN)
             ng[rows_b] += nt(stage_k[rows_b], kw[:, lanes]) + nt(stage_v[rows_b], vw[:, lanes])
 
@@ -295,22 +326,32 @@
     def tail_copy(i, t, j):
         lanes = pl.ds(pl.multiple_of(i * 2 * wide, 2 * wide), 2 * wide)
         return remote(
-            (qs, gs)[t].at[per_seq * (j + 1) - 1, :, lanes], tails.at[t, j, :, lanes],
+            heads.at[t, j, :, lanes], tails.at[t, j, :, lanes],
             tl_s.at[i, t, j], tl_r.at[i, t, j], after,
         )
 
-    def two_pairs(i, carry):
-        attend(2 * i, sa_k, sa_v, add_near(jnp.maximum(2 * i - 1, 0), sb_k, sb_v))
-        attend(2 * i + 1, sb_k, sb_v, add_near(2 * i, sa_k, sa_v))
-        for t in range(2):
-            for j in range(seqs):
-                tail_copy(i, t, j).start()
-        return carry
-
-    lax.fori_loop(0, hw // (2 * wide), two_pairs, 0)
-    last = add_near(hw // wide - 1, sb_k, sb_v)
-    for b in range(blocks):
-        last(b)
+    def half_of(every, at_last):
+        def two_pairs(i, carry):
+            attend(
+                every, 2 * i, sa_k, sa_v, add_near(every, jnp.maximum(2 * i - 1, 0), sb_k, sb_v)
+            )
+            attend(every, 2 * i + 1, sb_k, sb_v, add_near(every, 2 * i, sa_k, sa_v))
+            if at_last:
+                lanes = pl.ds(pl.multiple_of(i * 2 * wide, 2 * wide), 2 * wide)
+                for t, ref in enumerate((qs, gs)):
+                    for j in range(seqs):
+                        heads[t, j, :, lanes] = ref[place[per_seq * (j + 1) - 1], :, lanes]
+                        tail_copy(i, t, j).start()
+            return carry
+
+        lax.fori_loop(0, hw // (2 * wide), two_pairs, 0)
+        last = add_near(every, hw // wide - 1, sb_k, sb_v)
+        for step in range(2 * len(every)):
+            last(step)
+
+    for k in range(CAP):
+        arrive(k)
+        half_of([2 * k, 2 * k + 1], k == CAP - 1)
     for i in range(refs):
         db[pieces + i] = ng[i * NB_LEN : (i + 1) * NB_LEN].astype(BF)
     pl.semaphore_signal(free0, inc=1, device_id=sibling, device_id_type=MESH)
@@ -320,15 +361,16 @@
         copy.wait_send()
     return_copies = []
 
-    def give_back(r):
-        for k in range(CAP):
-            outb[CAP * r + k] = db[pieces + source[CAP * r + k]]
-        part = pl.ds(CAP * r, CAP)
+    def give_back(k, r):
+        here = k * near_by + r
+        outb[here] = db[pieces + source[k, r]]
         if r:
-            copy = remote(outb.at[part], returned.at[part], rt_s.at[r], rt_r.at[r], back(nz, r))
+            copy = remote(
+                outb.at[here], returned.at[here], rt_s.at[k, r], rt_r.at[k, r], back(nz, r)
+            )
             return_copies.append(copy)
         else:
-            copy = pltpu.make_async_copy(outb.at[part], returned.at[part], own_sem)
+            copy = pltpu.make_async_copy(outb.at[here], returned.at[here], own_sem.at[k])
             own_copies.append(copy)
         copy.start()
 
@@ -383,7 +425,8 @@
         phase1.append(out)
 
     for r in rels + [0]:
-        give_back(r)
+        for k in range(CAP):
+            give_back(k, r)
     outs = []
     for t, (ref, hbm) in enumerate(((qs, ctx_out), (gs, dq_out))):
         copy = pltpu.make_async_copy(ref, hbm, ld.at[6 + t])
@@ -478,7 +521,8 @@
         for j in range(seqs):
             tail = tails[t, j].astype(F32)
             tail = jnp.where(at_start, jnp.zeros_like(tail), tail)
-            own = [ref[per_seq * j + u].astype(F32) for u in range(per_seq)]
+            first = slots + 1 + per_seq * j
+            own = [ref[arrived[first + u]].astype(F32) for u in range(per_seq)]
             both = jnp.concatenate([tail] + own, axis=0)
             here[j] = pltpu.roll(both, rows + LAG, 0)[:rows].astype(BF)
     out[...] = jnp.zeros_like(out)
@@ -512,10 +556,10 @@
             jax.ShapeDtypeStruct((blocks, SPAN, width), BF),
             jax.ShapeDtypeStruct((2, seqs, SPAN, width), BF),
             jax.ShapeDtypeStruct((slots, NB_LEN, enc), BF),
-            jax.ShapeDtypeStruct((slots + 1,), jnp.int32),
+            jax.ShapeDtypeStruct((slots + 1 + blocks,), jnp.int32),
             jax.ShapeDtypeStruct((2 * PAD, width), F32),
         ),
-        in_specs=[smem] + [anywhere] * 5,
+        in_specs=[smem, smem] + [anywhere] * 5,
         out_specs=(anywhere, anywhere, anywhere, anywhere, smem, vmem),
         scratch_shapes=[
             pltpu.VMEM((database.shape[0], NB_LEN, enc), BF),
@@ -545,13 +589,13 @@
             dma((9,)),
             dma((n_dp,)),
             dma((n_dp,)),
-            dma((n_dp,)),
-            dma((n_dp,)),
+            dma((CAP, n_dp)),
+            dma((CAP, n_dp)),
             dma((2,)),
             dma((2,)),
-            dma,
-            dma((n_dp,)),
-            dma((n_dp,)),
+            dma((CAP,)),
+            dma((CAP, n_dp)),
+            dma((CAP, n_dp)),
             dma((width // (4 * HD), 2, seqs)),
             dma((width // (4 * HD), 2, seqs)),
             dma((chunks,)),
@@ -568,7 +612,15 @@
         compiler_params=pltpu.CompilerParams(
             collective_id=0, has_side_effects=True, vmem_limit_bytes=VMEM_LIMIT
         ),
-    )((shard * database.shape[0] + wanted).swapaxes(2, 3), database, queries, d_context, key_weight, value_weight)
+    )(
+        shard.swapaxes(2, 3),
+        wanted.swapaxes(2, 3),
+        database,
+        queries,
+        d_context,
+        key_weight,
+        value_weight,
+    )
     rows = 32
     per_dev = enc // (n_dp * n_seq)
     part = jax.ShapeDtypeStruct((per_dev, width), F32)

time: 141 us -> 144 us (1.021)
  Pallas kernels: 138 us -> 143 us
    pallas_call x1, Pallas kernels: 130 us -> 135 us  [local(): pl.pallas_call(functools.partial(main_kernel, nz, side), name='main', out...]
where the time goes in v4:
time: 144 us
  Pallas kernels  143 us (99%)
    pallas_call x1, Pallas kernels, local(): pl.pallas_call(functools.partial(main_kernel, nz, side), name='main', out...  135 us
    pallas_call x1, Pallas kernels, local(): pl.pallas_call(finish_kernel, name='finish', out_shape=(jax.ShapeDtypeStr...  8.24 us

profile of v4, /device:TPU:1, one launch (start us, length us, event | category | flops | bytes accessed | tf_op | source)
XLA Modules:
  0.0 143.8 jit_solution(14236887290361689023)
XLA Ops:
  0.6 134.7 %main.1 = (bf16[4,64,2048]{2,1,0:T(8,128)(2,1)}, bf16[4,64,2048]{2,1,0:T(8,128)(2,1)}, bf16[2,2,64,2048]{3,2,1,0:T(8,128)(2,1)}, bf16[16,128,896]{2,1,0:T(8,128)(2,1)}, s32[21]{0:T(128)}, /*index=5*/f32[16,2048]{1,0:T(8,128)}) custom-call(s32[1,1,2,4]{3,2,1,0:T(2,128)} %bitcast.2, s32[1,1,2,4]{3,2,1,0:T(2,128)} %bitcast.3, bf16[16,128,896]{2,1,0:T(8,128)(2,1)} %db_hbm.1, ...), custom_call_target="tpu_custom_call" | custom-call | tf_op jit(solution)/shard_map/main/pallas_call | solution.py:551
  135.4 8.2 %finish.1 = (f32[16,128,896]{2,1,0:T(8,128)}, f32[7,2048]{1,0:T(8,128)}, f32[7,2048]{1,0:T(8,128)}, bf16[2,128,2048]{2,1,0:T(8,128)(2,1)}, bf16[2,128,2048]{2,1,0:T(8,128)(2,1)}) custom-call(s32[21]{0:T(128)} %get-tuple-element.16.arrived, bf16[16,128,896]{2,1,0:T(8,128)(2,1)} %get-tuple-element.17.returned, f32[16,2048]{1,0:T(8,128)} %get-tuple-element.18.wgrad, ...), custom_call_target="tpu_custom_call" | custom-call | tf_op jit(solution)/shard_map/finish/pallas_call | solution.py:630

commit v5 on v4

--- a/solution.py
+++ b/solution.py
@@ -178,7 +178,8 @@
             copy = remote(
                 outb.at[here], inb.at[here], ga_s.at[k, r], ga_r.at[k, r], toward(nz, r)
             )
-            copy.start()
+            if k == 0:
+                copy.start()
             sends[k, r] = copy
     for k in range(CAP):
         row = jnp.clip(arr_s[0, 0, k], 0, last_row)
@@ -235,6 +236,11 @@
     loads[1].wait()
     loads[2].wait()
     step_lanes = 512
+
+    for r in first_sent:
+        for k in range(1, CAP):
+            sends[k - 1, r].wait_send()
+            sends[k, r].start()
 
     def arrive(k):
         for m in [0] + sorted(range(1, nz), key=lambda m: (-min(m, nz - m), m)):
@@ -357,8 +363,8 @@
     pl.semaphore_signal(free0, inc=1, device_id=sibling, device_id_type=MESH)
     for s in steps:
         pl.semaphore_signal(free1, inc=1, device_id=along(side, True, s), device_id_type=MESH)
-    for copy in sends.values():
-        copy.wait_send()
+    for r in rels:
+        sends[CAP - 1, r].wait_send()
     return_copies = []
 
     def give_back(k, r):

time: 144 us -> 144 us (level)
  no operation moved by 1% of the time
where the time goes in v5:
time: 144 us
  Pallas kernels  143 us (99%)
    pallas_call x1, Pallas kernels, local(): pl.pallas_call(functools.partial(main_kernel, nz, side), name='main', out...  135 us
    pallas_call x1, Pallas kernels, local(): pl.pallas_call(finish_kernel, name='finish', out_shape=(jax.ShapeDtypeStr...  8.24 us

profile of v5, /device:TPU:1, one launch (start us, length us, event | category | flops | bytes accessed | tf_op | source)
XLA Modules:
  0.0 143.8 jit_solution(12843324755159789657)
XLA Ops:
  0.6 134.8 %main.1 = (bf16[4,64,2048]{2,1,0:T(8,128)(2,1)}, bf16[4,64,2048]{2,1,0:T(8,128)(2,1)}, bf16[2,2,64,2048]{3,2,1,0:T(8,128)(2,1)}, bf16[16,128,896]{2,1,0:T(8,128)(2,1)}, s32[21]{0:T(128)}, /*index=5*/f32[16,2048]{1,0:T(8,128)}) custom-call(s32[1,1,2,4]{3,2,1,0:T(2,128)} %bitcast.2, s32[1,1,2,4]{3,2,1,0:T(2,128)} %bitcast.3, bf16[16,128,896]{2,1,0:T(8,128)(2,1)} %db_hbm.1, ...), custom_call_target="tpu_custom_call" | custom-call | tf_op jit(solution)/shard_map/main/pallas_call | solution.py:557
  135.4 8.2 %finish.1 = (f32[16,128,896]{2,1,0:T(8,128)}, f32[7,2048]{1,0:T(8,128)}, f32[7,2048]{1,0:T(8,128)}, bf16[2,128,2048]{2,1,0:T(8,128)(2,1)}, bf16[2,128,2048]{2,1,0:T(8,128)(2,1)}) custom-call(s32[21]{0:T(128)} %get-tuple-element.16.arrived, bf16[16,128,896]{2,1,0:T(8,128)(2,1)} %get-tuple-element.17.returned, f32[16,2048]{1,0:T(8,128)} %get-tuple-element.18.wgrad, ...), custom_call_target="tpu_custom_call" | custom-call | tf_op jit(solution)/shard_map/finish/pallas_call | solution.py:636
